TPU v7x, 32 devices: a whole 2x2x4 slice. The times are simulated.
32 devices in a mesh: cell: 32 (over z, y, x, core).
Axes of the slice: x: 2, y: 2, z: 4, core: 2. Of those that a mesh axis runs over, the one named last changes fastest.
Arguments:
- splats: float32 [9, 65536], P(None, 'cell'), may hold values from -6 to 20, as said below
- target: float32 [3, 131072], P(None, 'cell'), may hold values from 0 to 1
- slot_owner: int32 [512, 256, 1], P('cell'), may hold values from 0 to 31; in each aligned block of 4096 rows (0 to 4095, 4096 to 8191, ..., all dimensions but the last counted through in order) at most 256 rows name the same one
- slot_row: int32 [512, 256], P('cell'), may hold values from 0 to 2047
- depth_order: int32 [512, 256], P('cell'), may hold values from 0 to 255, each once within a row
- tile_count: int32 [512], P('cell'), may hold values from 64 to 256
Outputs:
- rendered: float32 [3, 131072], P(None, 'cell')
- grad_splats: float32 [9, 65536], P(None, 'cell')
Inputs may be any that keep to these rules, and one draw needn't show every extreme that they name: Rows of splats: mean x and y in tile pixels, entries a, b, c of the factor of the inverse covariance (a and c positive), opacity logit, red, green, blue. `slot_owner`: among the slots of one device's 16 tiles no cell is named more than 256 times; in some devices' tiles some cell is named exactly 256 times.
All inputs are finite; a program needn't handle non-finite values.
Results may differ from a plain program's by a relative error of at most 0.00021.
Values sent between devices are 32-bit elements; how exact they have to be, the bound alone decides.
A program may use at most 320 MiB of HBM per device.

v0:
```python
import jax
import jax.numpy as jnp
from jax import lax
from jax.sharding import PartitionSpec as P

SIDE = 16


def shade_tile(params, live_mask, target_tile):
    pixel_index = jnp.arange(SIDE * SIDE)
    pixel_x = (pixel_index % SIDE).astype(jnp.float32) + 0.5
    pixel_y = (pixel_index // SIDE).astype(jnp.float32) + 0.5
    diff_x = pixel_x[None, :] - params[0][:, None]
    diff_y = pixel_y[None, :] - params[1][:, None]
    first_axis = params[2][:, None] * diff_x + params[3][:, None] * diff_y
    second_axis = params[4][:, None] * diff_y
    opacity = jax.nn.sigmoid(params[5]) * live_mask
    alpha = opacity[:, None] * jnp.exp(-0.5 * (first_axis * first_axis + second_axis * second_axis))
    survive = 1.0 - alpha
    transmit = jnp.cumprod(survive, axis=0) / survive
    picture = jnp.dot(params[6:9], transmit * alpha, precision=lax.Precision.HIGHEST)
    error_sum = 0.5 * jnp.sum((picture - target_tile) ** 2)
    return (error_sum, picture)


def tile_gradient(params, live_mask, target_tile):
    (error_sum, picture), slot_grads = jax.value_and_grad(shade_tile, has_aux=True)(
        params, live_mask, target_tile
    )
    return (picture, slot_grads)


def per_device(splats, target, slot_owner, slot_row, depth_order, tile_count):
    cell_count = lax.axis_size("cell")
    rows_owned = splats.shape[1]
    tiles, block = slot_row.shape
    slot_total = tiles * block
    capacity = max(2, 2 * slot_total // cell_count)
    owners = jnp.take_along_axis(slot_owner[:, :, 0], depth_order, axis=1).reshape(-1)
    rows_local = jnp.take_along_axis(slot_row, depth_order, axis=1).reshape(-1)
    by_owner = jnp.argsort(owners, stable=True)
    counts = jnp.sum((owners[None, :] == jnp.arange(cell_count)[:, None]).astype(jnp.int32), axis=1)
    starts = jnp.cumsum(counts) - counts
    sorted_place = jnp.arange(slot_total) - starts[owners[by_owner]]
    position = jnp.zeros((slot_total,), jnp.int32).at[by_owner].set(sorted_place)
    bucket = owners * capacity + position
    asking = (
        jnp.zeros((cell_count * capacity,), jnp.int32)
        .at[bucket]
        .set(rows_local)
        .reshape(cell_count, capacity)
    )
    received = lax.all_to_all(asking, "cell", split_axis=0, concat_axis=0, tiled=True)
    shard_rows = lax.all_gather(splats, "cell", axis=1, tiled=True)
    owners_here = shard_rows.shape[1] // rows_owned
    shifted = jnp.arange(owners_here, dtype=jnp.int32)[:, None] * rows_owned
    columns = (asking + shifted).reshape(-1)
    values = jnp.take(shard_rows, columns, axis=1)
    params = jnp.take(values, bucket, axis=1)
    live_mask = (depth_order < tile_count[:, None]).astype(jnp.float32)
    targets = target.reshape(3, tiles, SIDE * SIDE)
    tile_params = params.reshape(9, tiles, block)
    pictures, grads = jax.vmap(tile_gradient, in_axes=(1, 0, 1), out_axes=(1, 1))(
        tile_params, live_mask, targets
    )
    rendered = pictures.reshape(3, -1)
    slot_grads = grads.reshape(9, -1)
    outgoing = jnp.zeros((9, cell_count * capacity), jnp.float32).at[:, bucket].set(slot_grads)
    incoming = lax.all_to_all(
        outgoing.reshape(9, cell_count, capacity), "cell", split_axis=1, concat_axis=1, tiled=True
    )
    grad_splats = (
        jnp.zeros((9, rows_owned), jnp.float32)
        .at[:, received.reshape(-1)]
        .add(incoming.reshape(9, -1))
    )
    return (rendered, grad_splats)


def solution(mesh):
    in_specs = (
        P(None, "cell"),
        P(None, "cell"),
        P("cell", None, None),
        P("cell", None),
        P("cell", None),
        P("cell"),
    )
    out_specs = (P(None, "cell"), P(None, "cell"))
    return jax.shard_map(
        per_device, mesh=mesh, in_specs=in_specs, out_specs=out_specs, check_vma=False
    )
```

profile of v0, /device:TPU:13, one launch (start us, length us, event | category | flops | bytes accessed | tf_op | source)
XLA Modules:
  0.0 695.9 jit_solution(18165704896469934756)
XLA Ops:
  10.3 32.8 %gather_fusion.4 = s32[4096]{0:T(1024)S(1)} fusion(s32[16,256]{1,0:T(8,128)S(1)} %copy-done, s32[4096]{0:T(1024)S(1)} %bitcast.91), kind=kCustom, calls=%fused_computation.1.clone | custom fusion | bytes 65536 | tf_op jit(solution)/shard_map/jit(take_along_axis)/gather | solution.py:40
  43.1 32.8 %gather_fusion.3 = s32[4096]{0:T(1024)S(1)} fusion(s32[16,256]{1,0:T(8,128)S(1)} %bitcast.90, s32[4096]{0:T(1024)S(1)} %bitcast.92), kind=kCustom, calls=%fused_computation.clone | custom fusion | bytes 65536 | tf_op jit(solution)/shard_map/jit(take_along_axis)/gather | solution.py:39
  82.2 23.0 %gather_fusion = s32[4096]{0:T(1024)S(1)} fusion(s32[4096]{0:T(1024)S(1)} %bitcast.88, s32[4096]{0:T(1024)S(1)} %get-tuple-element.112), kind=kCustom, calls=%fused_computation.2 | custom fusion | bytes 49152 | tf_op jit(solution)/shard_map/gather | solution.py:44
  112.5 15.6 %select_subtract_fusion = s32[4096]{0:T(1024)S(1)} fusion(pred[4096]{0:T(1024)(128)(4,1)S(1)} %get-tuple-element.53, pred[4096]{0:T(1024)(128)(4,1)S(1)} %get-tuple-element.52, pred[4096]{0:T(1024)(128)(4,1)S(1)} %get-tuple-element.51, pred[4096]{0:T(1024)(128)(4,1)S(1)} %get-tuple-element.50, pred[4096]{0:T(1024)(128)(4,1)S(1)} %get-tuple-element.49, ...), kind=kLoop, calls=%fused_computation.155 | loop fusion | flops 106496 | bytes 135268 | tf_op jit(solution)/shard_map/sub | solution.py:44
  128.1 15.5 %scatter_custom_fusion = s32[4096]{0:T(1024)S(1)} fusion(s32[4096]{0:T(1024)S(1)} %get-tuple-element.113, s32[4096]{0:T(1024)S(1)} %select_subtract_fusion, s32[]{:T(128)} %constant.71.clone.1), kind=kCustom, calls=%fused_computation.172 | custom fusion | bytes 16388 | tf_op jit(solution)/shard_map/scatter | solution.py:45
  143.7 16.1 %scatter_custom_fusion.1 = s32[8192]{0:T(1024)} fusion(s32[4096]{0:T(1024)S(1)} %get-tuple-element.71, s32[4096]{0:T(1024)S(1)} %bitcast.105, s32[]{:T(128)} %constant.71.clone.1), kind=kCustom, calls=%fused_computation.157 | custom fusion | bytes 32772 | tf_op jit(solution)/shard_map/scatter | solution.py:50
  167.8 37.6 %all-gather.2.cloned.1.call-done = f32[9,65536]{0,1:T(8,128)} async-done(((f32[9,2048]{0,1:T(8,128)}), f32[9,65536]{0,1:T(8,128)}) %all-gather.2.cloned.1.call-update) | async-done | bytes 2359312 | tf_op jit(solution)/shard_map/all_gather | solution.py:54
  205.5 38.2 %gather_fusion.1 = f32[8192,9]{1,0:T(8,128)} fusion(f32[9,65536]{0,1:T(8,128)} %all-gather.2.cloned.1.call-done, s32[8192]{0:T(1024)S(1)} %broadcast_clamp_fusion), kind=kCustom, calls=%fused_computation.3 | custom fusion | bytes 622592 | tf_op jit(solution)/shard_map/jit(_take)/gather | solution.py:58
  243.7 7.5 %select_bitcast_fusion = f32[9,8192]{0,1:T(8,128)} fusion(f32[8192,9]{1,0:T(8,128)} %gather_fusion.1, pred[8192]{0:T(1024)(128)(4,1)S(1)} %compare_and_fusion), kind=kLoop, calls=%fused_computation.28 | loop fusion | flops 73728 | bytes 598016 | tf_op jit(solution)/shard_map/jit(_take)/select_n | solution.py:58
  251.2 13.0 %gather_fusion.2 = f32[4096,9]{1,0:T(8,128)S(1)} fusion(f32[9,8192]{0,1:T(8,128)} %select_bitcast_fusion, s32[4096]{0:T(1024)S(1)} %broadcast_clamp_fusion.1), kind=kCustom, calls=%fused_computation.4 | custom fusion | bytes 311296 | tf_op jit(solution)/shard_map/jit(_take)/gather | solution.py:59
  272.9 9.9 %slice.300 = f32[16,127,256]{2,1,0:T(8,128)} slice(f32[16,256,256]{2,1,0:T(8,128)} %multiply_subtract_fusion), slice={[0:16:1], [2:256:2], [0:256:1]} | slice | bytes 4161536 | tf_op jit(solution)/shard_map/vmap(jvp(jit(cumprod)))/jvp()/slice | solution.py:20
  282.8 9.8 %slice.265 = f32[16,128,256]{2,1,0:T(8,128)} slice(f32[16,256,256]{2,1,0:T(8,128)} %multiply_subtract_fusion), slice={[0:16:1], [0:255:2], [0:256:1]} | slice | bytes 4194304 | tf_op jit(solution)/shard_map/vmap(jvp(jit(cumprod)))/jvp()/slice | solution.py:20
  292.6 8.1 %slice.266 = f32[16,128,256]{2,1,0:T(8,128)S(1)} slice(f32[16,256,256]{2,1,0:T(8,128)} %multiply_subtract_fusion), slice={[0:16:1], [1:256:2], [0:256:1]} | slice | bytes 4194304 | tf_op jit(solution)/shard_map/vmap(jvp(jit(cumprod)))/jvp()/slice | solution.py:20
  363.3 10.4 %pad.331 = f32[16,128,256]{2,1,0:T(8,128)} pad(f32[16,64,256]{2,1,0:T(8,128)} %pad_maximum_fusion.1, f32[]{:T(128)} %constant.101.clone.1), padding=0_0_0x0_1_1x0_0_0 | pad | bytes 3145732 | tf_op jit(solution)/shard_map/vmap(jvp(jit(cumprod)))/jvp()/pad | solution.py:20
  379.4 11.9 %pad.333 = f32[16,256,256]{2,1,0:T(8,128)} pad(f32[16,128,256]{2,1,0:T(8,128)} %pad_maximum_fusion, f32[]{:T(128)} %constant.101.clone.1), padding=0_0_0x0_1_1x0_0_0 | pad | bytes 6291460 | tf_op jit(solution)/shard_map/vmap(jvp(jit(cumprod)))/jvp()/pad | solution.py:20
  391.3 11.9 %pad.334 = f32[16,256,256]{2,1,0:T(8,128)} pad(f32[16,128,256]{2,1,0:T(8,128)} %add.284, f32[]{:T(128)} %constant.101.clone.1), padding=0_0_0x1_0_1x0_0_0 | pad | bytes 6291460 | tf_op jit(solution)/shard_map/vmap(jvp(jit(cumprod)))/jvp()/pad | solution.py:20
  413.0 8.5 %fusion.13 = (f32[16,256,256]{2,1,0:T(8,128)S(1)}, f32[16,256,256]{2,1,0:T(8,128)}) fusion(f32[16,256]{1,0:T(8,128)S(1)} %mul.339, f32[16,256]{1,0:T(8,128)S(1)} %copy-done.63, f32[256]{0:T(256)S(1)} %copy-done.94, f32[16,256]{1,0:T(8,128)S(1)} %copy-done.67, f32[16,256]{1,0:T(8,128)S(1)} %copy-done.71, f32[256]{0:T(256)S(1)} %copy-done.98, ...), kind=kOutput, calls=%fused_computation.37 | convolution fusion | flops 52441088 | bytes 8636416 | tf_op jit(solution)/shard_map/vmap(transpose(jvp()))/dot_general | solution.py:21
  425.5 9.8 %slice.302 = f32[16,128,256]{2,1,0:T(8,128)} slice(f32[16,255,256]{2,1,0:T(8,128)} %get-tuple-element.77), slice={[0:16:1], [0:255:2], [0:256:1]} | slice | bytes 4194304 | tf_op jit(solution)/shard_map/vmap(transpose(jvp(jit(cumprod))))/jvp()/slice | solution.py:20
  435.3 9.8 %slice.301 = f32[16,128,256]{2,1,0:T(8,128)} slice(f32[16,255,256]{2,1,0:T(8,128)} %get-tuple-element.76), slice={[0:16:1], [0:255:2], [0:256:1]} | slice | bytes 4194304 | tf_op jit(solution)/shard_map/vmap(transpose(jvp(jit(cumprod))))/jvp()/slice | solution.py:20
  477.9 8.2 %fusion.16 = f32[16,3,256]{2,1,0:T(4,128)S(1)} fusion(f32[16,256]{1,0:T(8,128)S(1)} %mul.339, f32[16,256]{1,0:T(8,128)S(1)} %copy-done.64, f32[256]{0:T(256)S(1)} %copy-done.95, f32[16,256]{1,0:T(8,128)S(1)} %copy-done.68, f32[16,256]{1,0:T(8,128)S(1)} %copy-done.72, f32[256]{0:T(256)S(1)} %copy-done.99, f32[16,256]{1,0:T(8,128)S(1)} %copy-done.76, ...), kind=kOutput, calls=%fused_computation.46 | convolution fusion | flops 52441088 | bytes 4442112 | tf_op jit(solution)/shard_map/vmap(transpose(jvp()))/dot_general | solution.py:21
  489.7 8.8 %pad.353 = f32[16,32,256]{2,1,0:T(8,128)} pad(f32[16,15,256]{2,1,0:T(8,128)} %get-tuple-element.90, f32[]{:T(128)} %constant.101.clone.1), padding=0_0_0x2_1_1x0_0_0 | pad | bytes 770052 | tf_op jit(solution)/shard_map/vmap(transpose(jvp(jit(cumprod))))/jvp()/pad | solution.py:20
  500.9 9.3 %pad.383 = f32[16,64,256]{2,1,0:T(8,128)} pad(f32[16,32,256]{2,1,0:T(8,128)} %get-tuple-element.58, f32[]{:T(128)} %constant.101.clone.1), padding=0_0_0x1_0_1x0_0_0 | pad | bytes 1572868 | tf_op jit(solution)/shard_map/vmap(transpose(jvp(jit(cumprod))))/jvp()/pad | solution.py:20
  510.2 9.3 %pad.348 = f32[16,64,256]{2,1,0:T(8,128)} pad(f32[16,31,256]{2,1,0:T(8,128)} %get-tuple-element.86, f32[]{:T(128)} %constant.101.clone.1), padding=0_0_0x2_1_1x0_0_0 | pad | bytes 1556484 | tf_op jit(solution)/shard_map/vmap(transpose(jvp(jit(cumprod))))/jvp()/pad | solution.py:20
  529.3 10.4 %pad.385 = f32[16,128,256]{2,1,0:T(8,128)} pad(f32[16,64,256]{2,1,0:T(8,128)} %get-tuple-element.56, f32[]{:T(128)} %constant.101.clone.1), padding=0_0_0x1_0_1x0_0_0 | pad | bytes 3145732 | tf_op jit(solution)/shard_map/vmap(transpose(jvp(jit(cumprod))))/jvp()/pad | solution.py:20
  539.8 10.4 %pad.343 = f32[16,128,256]{2,1,0:T(8,128)} pad(f32[16,63,256]{2,1,0:T(8,128)} %get-tuple-element.82, f32[]{:T(128)} %constant.101.clone.1), padding=0_0_0x2_1_1x0_0_0 | pad | bytes 3129348 | tf_op jit(solution)/shard_map/vmap(transpose(jvp(jit(cumprod))))/jvp()/pad | solution.py:20
  555.4 8.0 %pad.388 = f32[16,256,256]{2,1,0:T(8,128)} pad(f32[16,128,256]{2,1,0:T(8,128)S(1)} %mul.395, f32[]{:T(128)} %constant.101.clone.1), padding=0_0_0x0_1_1x0_0_0 | pad | bytes 6291460 | tf_op jit(solution)/shard_map/vmap(transpose(jvp(jit(cumprod))))/jvp()/pad | solution.py:20
  563.4 12.0 %pad.387 = f32[16,256,256]{2,1,0:T(8,128)} pad(f32[16,128,256]{2,1,0:T(8,128)} %get-tuple-element.54, f32[]{:T(128)} %constant.101.clone.1), padding=0_0_0x1_0_1x0_0_0 | pad | bytes 6291460 | tf_op jit(solution)/shard_map/vmap(transpose(jvp(jit(cumprod))))/jvp()/pad | solution.py:20
  575.5 8.1 %pad.338 = f32[16,256,256]{2,1,0:T(8,128)} pad(f32[16,127,256]{2,1,0:T(8,128)S(1)} %copy-done.16, f32[]{:T(128)} %constant.101.clone.1), padding=0_0_0x2_1_1x0_0_0 | pad | bytes 6275076 | tf_op jit(solution)/shard_map/vmap(transpose(jvp(jit(cumprod))))/jvp()/pad | solution.py:20
  583.7 12.1 %fusion.11 = (f32[16,256]{1,0:T(8,128)S(1)}, f32[16,256]{1,0:T(8,128)S(1)}, f32[16,256]{1,0:T(8,128)S(1)}, f32[16,256]{1,0:T(8,128)S(1)}, f32[16,256]{1,0:T(8,128)S(1)}, /*index=5*/f32[16,256]{1,0:T(8,128)S(1)}) fusion(f32[16,256]{1,0:T(8,128)S(1)} %copy-done.61, f32[16,256]{1,0:T(8,128)S(1)} %copy-done.65, f32[256]{0:T(256)S(1)} %copy-done.96, ...), kind=kLoop, calls=%fused_computation.26 | loop fusion | flops 49258496 | bytes 21186560 | tf_op jit(solution)/shard_map/vmap(transpose(jvp()))/reduce_sum | solution.py:16
  597.1 13.2 %scatter_custom_fusion.2 = f32[9,8192]{0,1:T(8,128)} fusion(s32[4096]{0:T(1024)} %copy-done.90, f32[4096,9]{1,0:T(8,128)S(1)} %copy.56, f32[]{:T(128)} %constant.101.clone.1), kind=kCustom, calls=%fused_computation.42 | custom fusion | bytes 295424 | tf_op jit(solution)/shard_map/scatter | solution.py:68
  619.6 13.0 %all-to-all-done.1 = f32[9,32,256]{2,0,1:T(8,128)S(1)} async-done(((f32[9,32,256]{2,0,1:T(8,128)}), f32[9,32,256]{2,0,1:T(8,128)S(1)}, u32[]{:S(2)}, u32[]{:S(2)}) %all-to-all-start.1) | async-done | bytes 294944 | tf_op jit(solution)/shard_map/all_to_all | solution.py:69
  635.8 52.3 %scatter_custom_fusion.3 = f32[9,2048]{0,1:T(8,128)S(1)} fusion(s32[8192]{0:T(1024)S(1)} %bitcast.104, f32[8192,9]{1,0:T(8,128)} %copy.59, f32[]{:T(128)} %constant.101.clone.1), kind=kCustom, calls=%fused_computation.59 | custom fusion | flops 73728 | bytes 74240 | tf_op jit(solution)/shard_map/scatter-add | solution.py:75
  (413 shorter events, 182.3 us)
Async XLA Ops:
  7.2 198.3 %all-gather.2.cloned.1.call-start = ((), (), s32[]{:S(2)}) async-start(), calls=%async_computation.2 | async-start | bytes 34603008 | tf_op jit(solution)/shard_map/all_gather | solution.py:54
  10.3 32.8 %copy-start.91 = (s32[16,256,1]{1,2,0:T(1,128)S(1)}, s32[16,256,1]{1,2,0:T(1,128)}, u32[]{:S(2)}) copy-start(s32[16,256,1]{1,2,0:T(1,128)} %param.10) | copy-start | bytes 49156
  43.1 32.8 %copy-start.82 = (s32[16,256]{1,0:T(8,128)S(1)}, s32[16,256]{1,0:T(8,128)}, u32[]{:S(2)}) copy-start(s32[16,256]{1,0:T(8,128)} %param.12) | copy-start | bytes 49156
  143.6 22.6 %copy-start.90 = (s32[4096]{0:T(1024)}, s32[4096]{0:T(1024)S(1)}, u32[]{:S(2)}) copy-start(s32[4096]{0:T(1024)S(1)} %get-tuple-element.71) | copy-start | bytes 49156
  159.7 454.1 %all-to-all-start = ((s32[32,1,256]{2,1,0:T(1,128)}), s32[32,1,256]{2,1,0:T(1,128)}, u32[]{:S(2)}, u32[]{:S(2)}) async-start(s32[32,1,256]{2,1,0:T(1,128)} %bitcast.42), calls=%async_computation | async-start | bytes 65536 | tf_op jit(solution)/shard_map/all_to_all | solution.py:53
  166.2 100.3 %copy-start.93 = (f32[256]{0:T(256)}, f32[256]{0:T(256)S(1)}, u32[]{:S(2)}) copy-start(f32[256]{0:T(256)S(1)} %get-tuple-element.148) | copy-start | bytes 3076
  166.3 100.3 %copy-start.97 = (f32[256]{0:T(256)}, f32[256]{0:T(256)S(1)}, u32[]{:S(2)}) copy-start(f32[256]{0:T(256)S(1)} %get-tuple-element.149) | copy-start | bytes 3076
  251.2 14.7 %copy-start.101 = (s32[16]{0:T(128)S(1)}, s32[16]{0:T(128)}, u32[]{:S(2)}) copy-start(s32[16]{0:T(128)} %param.13) | copy-start | bytes 196
  265.8 211.9 %copy-start.60 = (f32[16,256]{1,0:T(8,128)}, f32[16,256]{1,0:T(8,128)S(1)}, u32[]{:S(2)}) copy-start(f32[16,256]{1,0:T(8,128)S(1)} %mul.339) | copy-start | bytes 49156
  265.8 17.0 %copy-start.62 = (f32[16,256]{1,0:T(8,128)}, f32[16,256]{1,0:T(8,128)S(1)}, u32[]{:S(2)}) copy-start(f32[16,256]{1,0:T(8,128)S(1)} %sub.59) | copy-start | bytes 49156
  265.8 17.0 %copy-start.66 = (f32[16,256]{1,0:T(8,128)}, f32[16,256]{1,0:T(8,128)S(1)}, u32[]{:S(2)}) copy-start(f32[16,256]{1,0:T(8,128)S(1)} %mul.335) | copy-start | bytes 49156
  265.8 16.9 %copy-start.70 = (f32[16,256]{1,0:T(8,128)}, f32[16,256]{1,0:T(8,128)S(1)}, u32[]{:S(2)}) copy-start(f32[16,256]{1,0:T(8,128)S(1)} %sub.54) | copy-start | bytes 49156
  265.9 16.9 %copy-start.74 = (f32[16,256]{1,0:T(8,128)}, f32[16,256]{1,0:T(8,128)S(1)}, u32[]{:S(2)}) copy-start(f32[16,256]{1,0:T(8,128)S(1)} %mul.332) | copy-start | bytes 49156
  265.9 16.9 %copy-start.83 = (f32[16,256]{1,0:T(8,128)}, f32[16,256]{1,0:T(8,128)S(1)}, u32[]{:S(2)}) copy-start(f32[16,256]{1,0:T(8,128)S(1)} %div.24) | copy-start | bytes 49156
  314.2 15.5 %copy-start.11 = (f32[16,64,256]{2,1,0:T(8,128)}, f32[16,64,256]{2,1,0:T(8,128)S(1)}, u32[]{:S(2)}) copy-start(f32[16,64,256]{2,1,0:T(8,128)S(1)} %slice.269) | copy-start | bytes 3145732
  318.4 22.4 %copy-start.10 = (f32[16,128,256]{2,1,0:T(8,128)S(1)}, f32[16,128,256]{2,1,0:T(8,128)}, u32[]{:S(2)}) copy-start(f32[16,128,256]{2,1,0:T(8,128)} %mul.345) | copy-start | bytes 6291460
  331.6 15.9 %copy-start.29 = (f32[16,16,256]{2,1,0:T(8,128)}, f32[16,16,256]{2,1,0:T(8,128)S(1)}, u32[]{:S(2)}) copy-start(f32[16,16,256]{2,1,0:T(8,128)S(1)} %slice.275) | copy-start | bytes 786436
  332.8 15.8 %copy-start.40 = (f32[16,7,256]{2,1,0:T(8,128)}, f32[16,7,256]{2,1,0:T(8,128)S(1)}, u32[]{:S(2)}) copy-start(f32[16,7,256]{2,1,0:T(8,128)S(1)} %slice.292) | copy-start | bytes 344068
  332.9 15.7 %copy-start.38 = (f32[16,8,256]{2,1,0:T(8,128)}, f32[16,8,256]{2,1,0:T(8,128)S(1)}, u32[]{:S(2)}) copy-start(f32[16,8,256]{2,1,0:T(8,128)S(1)} %slice.277) | copy-start | bytes 393220
  333.0 15.7 %copy-start.36 = (f32[16,8,256]{2,1,0:T(8,128)}, f32[16,8,256]{2,1,0:T(8,128)S(1)}, u32[]{:S(2)}) copy-start(f32[16,8,256]{2,1,0:T(8,128)S(1)} %slice.278) | copy-start | bytes 393220
  333.2 15.6 %copy-start.47 = (f32[16,4,256]{2,1,0:T(4,128)}, f32[16,4,256]{2,1,0:T(4,128)S(1)}, u32[]{:S(2)}) copy-start(f32[16,4,256]{2,1,0:T(4,128)S(1)} %slice.280) | copy-start | bytes 196612
  333.3 15.5 %copy-start.49 = (f32[16,4,256]{2,1,0:T(4,128)}, f32[16,4,256]{2,1,0:T(4,128)S(1)}, u32[]{:S(2)}) copy-start(f32[16,4,256]{2,1,0:T(4,128)S(1)} %slice.281) | copy-start | bytes 196612
  333.5 12.8 %copy-start.58 = (f32[16,2,256]{2,1,0:T(2,128)}, f32[16,2,256]{2,1,0:T(2,128)S(1)}, u32[]{:S(2)}) copy-start(f32[16,2,256]{2,1,0:T(2,128)S(1)} %slice.283) | copy-start | bytes 98308
  333.6 15.2 %copy-start.54 = (f32[16,2,256]{2,1,0:T(2,128)}, f32[16,2,256]{2,1,0:T(2,128)S(1)}, u32[]{:S(2)}) copy-start(f32[16,2,256]{2,1,0:T(2,128)S(1)} %slice.284) | copy-start | bytes 98308
  333.6 15.2 %copy-start.56 = (f32[16,2,256]{2,1,0:T(2,128)}, f32[16,2,256]{2,1,0:T(2,128)S(1)}, u32[]{:S(2)}) copy-start(f32[16,2,256]{2,1,0:T(2,128)S(1)} %mul.351) | copy-start | bytes 98308
  334.5 14.3 %copy-start.51 = (f32[16,3,256]{2,1,0:T(4,128)}, f32[16,3,256]{2,1,0:T(4,128)S(1)}, u32[]{:S(2)}) copy-start(f32[16,3,256]{2,1,0:T(4,128)S(1)} %slice.290) | copy-start | bytes 147460
  498.4 21.1 %copy-start.13 = (f32[16,64,256]{2,1,0:T(8,128)S(1)}, f32[16,64,256]{2,1,0:T(8,128)}, u32[]{:S(2)}) copy-start(f32[16,64,256]{2,1,0:T(8,128)} %slice.268) | copy-start | bytes 3145732
  522.6 27.6 %copy-start.5 = (f32[16,128,256]{2,1,0:T(8,128)S(1)}, f32[16,128,256]{2,1,0:T(8,128)}, u32[]{:S(2)}) copy-start(f32[16,128,256]{2,1,0:T(8,128)} %slice.265) | copy-start | bytes 6291460
  583.6 12.2 %copy-start.84 = (f32[16,256]{1,0:T(8,128)S(1)}, f32[16,256]{1,0:T(8,128)}, u32[]{:S(2)}) copy-start(f32[16,256]{1,0:T(8,128)} %copy-done.83) | copy-start | bytes 49156
  583.7 12.2 %copy-start.92 = (pred[16,256]{1,0:T(8,128)(4,1)S(1)}, pred[16,256]{1,0:T(8,128)(4,1)}, u32[]{:S(2)}) copy-start(pred[16,256]{1,0:T(8,128)(4,1)} %get-tuple-element.69) | copy-start | bytes 12292
  613.8 18.8 %all-to-all-start.1 = ((f32[9,32,256]{2,0,1:T(8,128)}), f32[9,32,256]{2,0,1:T(8,128)S(1)}, u32[]{:S(2)}, u32[]{:S(2)}) async-start(f32[9,32,256]{2,0,1:T(8,128)} %copy.57), calls=%async_computation.1 | async-start | bytes 1048576 | tf_op jit(solution)/shard_map/all_to_all | solution.py:69
  632.8 56.3 %copy-start.1 = (s32[16,256]{1,0:T(8,128)S(1)}, s32[16,256]{1,0:T(8,128)}, u32[]{:S(2)}) copy-start(s32[16,256]{1,0:T(8,128)} %param.11) | copy-start | bytes 49156
  (79 other events, 437.9 us)
Sparse Core Ops, SparseCore 0:
  10.9 194.5 all-gather.1
where the time goes:
time: 708 us; the launch traced here: 696 us
  local copies, waits for them, and re-layouts  437 us (62%)
  other arithmetic  158 us (22%)
  waiting for transfers between devices  50.6 us (7%)
  matrix products  22.3 us (3%)
  between operations  16.3 us (2%)
  starting transfers between devices  11.5 us (2%)
    pad x41, local copies, waits for them, and re-layouts, shade_tile(): transmit = jnp.cumprod(survive, axis=0) / survive  136 us
    slice x40, local copies, waits for them, and re-layouts, shade_tile(): transmit = jnp.cumprod(survive, axis=0) / survive  97.3 us
    scatter-add x1, other arithmetic, per_device(): grad_splats = jnp.zeros((9, rows_owned), jnp.float32).at[:, received.resh...  52.3 us
    gather x1, local copies, waits for them, and re-layouts, per_device(): values = jnp.take(shard_rows, columns, axis=1)  38.2 us
    all_gather x1, waiting for transfers between devices, per_device(): shard_rows = lax.all_gather(splats, 'cell', axis=1, tiled=True)  37.6 us
    gather x2, local copies, waits for them, and re-layouts, per_device(): rows_local = jnp.take_along_axis(slot_row, depth_order, axis=1).reshape(-1)  32.8 us
    gather x2, local copies, waits for them, and re-layouts, per_device(): jnp.take_along_axis(slot_owner[:, :, 0], depth_order, axis=1).reshape(-1)  32.8 us
    mul x34, other arithmetic, shade_tile(): transmit = jnp.cumprod(survive, axis=0) / survive  32.3 us
  transfers between devices with their start and end apart: 3, of which 2 were waited for; matrix products, arithmetic and copies ran while one was open for 80% of the time, Pallas kernels for 0%

commit v1 on v0

v1 whole, which is shorter than its diff:
```python
import functools

import jax
import jax.numpy as jnp
from jax import lax
from jax.experimental import pallas as pl
from jax.experimental.pallas import tpu as pltpu
from jax.sharding import PartitionSpec as P

SIDE = 16
PIX = SIDE * SIDE
ROWS = 16
PARAMS = 9
LANES = 128
F32, BF16, I32 = jnp.float32, jnp.bfloat16, jnp.int32
NT = (((1,), (1,)), ((), ()))
TN = (((0,), (0,)), ((), ()))


def split(x, parts):
    out = []
    for part in range(parts):
        out.append(x.astype(BF16))
        if part < parts - 1:
            x = x - out[-1].astype(F32)
    return out


def dot(a, b, dims=(((1,), (0,)), ((), ()))):
    return lax.dot_general(a, b, dims, preferred_element_type=F32)


def iota(shape, axis):
    return lax.broadcasted_iota(I32, shape, axis)


def one_hot(index, count):
    return jnp.where(iota((count, index.shape[1]), 0) == index, 1.0, 0.0)


def pad_rows(pieces, count):
    have = sum(piece.shape[0] for piece in pieces)
    if have < count:
        pieces = list(pieces) + [jnp.zeros((count - have, pieces[0].shape[1]), F32)]
    return jnp.concatenate(pieces, axis=0)


def plan_slots(order_ref, owner_ref, row_ref, own_ref, pos_ref, ask_ref, parts_ref):
    tiles, block = order_ref.shape
    cells, cap = ask_ref.shape
    before = jnp.where(iota((block, block), 0) < iota((block, block), 1), 1.0, 0.0).astype(BF16)
    parts_ref[...] = jnp.zeros_like(parts_ref)

    def tile(t, seen):
        at = pl.ds(t, 1)
        chosen = one_hot(order_ref[at, :], block).astype(BF16)
        row = row_ref[at, :]
        source = pad_rows(
            [owner_ref[at, :].astype(F32), (row >> 8).astype(F32), (row & 255).astype(F32)], 16
        )
        moved = dot(source.astype(BF16), chosen)
        own = moved[0:1].astype(I32)
        mine = one_hot(own, cells)
        earlier = dot(mine.astype(BF16), before) + seen
        pos = jnp.sum(mine * earlier, axis=0, keepdims=True).astype(I32)
        own_ref[at, :] = own
        pos_ref[at, :] = pos
        asked = jnp.concatenate([mine * moved[1:2], mine * moved[2:3]], axis=0).astype(BF16)
        parts_ref[...] += dot(asked, one_hot(pos, cap).astype(BF16), NT)
        return seen + jnp.sum(mine, axis=1, keepdims=True)

    lax.fori_loop(0, tiles, tile, jnp.zeros((cells, 1), F32))
    both = parts_ref[...].astype(I32)
    ask_ref[...] = both[:cells] * 256 + both[cells:]


def answer(splats_ref, rows_ref, values_ref):
    cells, cap = rows_ref.shape
    groups = splats_ref.shape[1] // LANES
    table = jnp.concatenate(
        [pad_rows([splats_ref[:, g * LANES : (g + 1) * LANES]], ROWS) for g in range(groups)], axis=0
    )
    table = jnp.concatenate(split(table, 3), axis=1)

    def cell(c, carry):
        row = rows_ref[pl.ds(c, 1), :]
        low = one_hot(row & (LANES - 1), LANES).astype(BF16)
        found = dot(table, jnp.concatenate([low, low, low], axis=0))
        high = row // LANES
        total = jnp.zeros((ROWS, cap), F32)
        for g in range(groups):
            total += jnp.where(high == g, found[g * ROWS : (g + 1) * ROWS], 0.0)
        values_ref[pl.ds(c, 1)] = total[None]
        return carry

    lax.fori_loop(0, cells, cell, 0)


def scan_rows(x, keep, fill, down, combine):
    at = iota(x.shape, 0)

    def moved(y, by):
        if down:
            return jnp.where(at >= by, pltpu.roll(y, by, 0), fill)
        return jnp.where(at < 8 - by, pltpu.roll(y, 8 - by, 0), fill)

    x = moved(x, 1)
    for by in (1, 2, 4):
        x = combine(x, moved(x, by))
    return x


def shade(
    values_ref, own_ref, pos_ref, order_ref, count_ref, target_ref, rendered_ref, out_ref,
    table_ref, f1_ref, f2_ref, alpha_ref, w_ref, h_ref,
):
    tiles, block = own_ref.shape
    cells, _, cap = values_ref.shape
    steps = block // 8
    pixel = iota((1, PIX), 1)
    x = (pixel % SIDE).astype(F32) + (0.5 - SIDE / 2)
    y = (pixel // SIDE).astype(F32) + (0.5 - SIDE / 2)
    one, zero = jnp.ones((1, PIX), F32), jnp.zeros((1, PIX), F32)
    linear = jnp.concatenate(
        [
            pad_rows([x, y, one], 8),
            pad_rows([zero, zero, zero, y, one], 8),
            pad_rows([zero, zero, zero, zero, zero, one], 8),
        ],
        axis=1,
    )
    linear = pad_rows([linear, linear, linear], 32).astype(BF16)
    moments = pad_rows([one, x, y], 16).astype(BF16)

    for c in range(cells):
        for part, piece in enumerate(split(values_ref[c], 3)):
            table_ref[c * ROWS : (c + 1) * ROWS, part * cap : (part + 1) * cap] = piece
    out_ref[...] = jnp.zeros_like(out_ref)

    def tile(t, carry):
        at = pl.ds(t, 1)
        own = own_ref[at, :]
        place = one_hot(pos_ref[at, :], cap).astype(BF16)
        found = dot(table_ref[...], jnp.concatenate([place, place, place], axis=0))
        p = jnp.zeros((ROWS, block), F32)
        for c in range(cells):
            p += jnp.where(own == c, found[c * ROWS : (c + 1) * ROWS], 0.0)
        live = jnp.where(order_ref[at, :] < count_ref[at, :], 1.0, 0.0)
        mx, my = p[0:1] - SIDE / 2, p[1:2] - SIDE / 2
        a, b, c2 = p[2:3], p[3:4], p[4:5]
        colour = p[6:9]
        sig = 1.0 / (1.0 + jnp.exp(-p[5:6]))
        unsig = 1.0 / (1.0 + jnp.exp(p[5:6]))
        factors = pad_rows([a, b, -(a * mx + b * my), c2, -(c2 * my), sig * live], 8)
        factors = pad_rows([z.astype(F32) for z in split(factors, 3)], 32).astype(BF16)
        spread = dot(factors, linear, TN)
        f1, f2 = spread[:, :PIX], spread[:, PIX : 2 * PIX]
        f1_ref[...] = f1
        f2_ref[...] = f2
        alpha_ref[...] = spread[:, 2 * PIX :] * jnp.exp(-0.5 * (f1 * f1 + f2 * f2))

        run = jnp.ones((8, PIX), F32)
        for v in range(steps):
            alpha = alpha_ref[8 * v : 8 * v + 8, :]
            w_ref[8 * v : 8 * v + 8, :] = run * alpha
            run = run * (1.0 - alpha)
        ahead = scan_rows(run, None, 1.0, True, lambda u, w: u * w)
        for v in range(steps):
            w_ref[8 * v : 8 * v + 8, :] *= ahead

        colours = [z.astype(F32) for z in split(colour, 3)]
        ch, cm, cl = colours
        wh, wl = split(w_ref[...], 2)
        stacked = pad_rows(colours, 16).astype(BF16)
        picture = dot(stacked, wh) + dot(stacked, wl)
        picture = picture[0:3] + picture[3:6] + picture[6:9]
        lanes = pl.ds(pl.multiple_of(t * PIX, PIX), PIX)
        rendered_ref[:, lanes] = picture
        error = picture - target_ref[:, lanes]
        errors = [z.astype(F32) for z in split(error, 3)]
        eh, em, el = errors
        dw = dot(
            pad_rows([ch, ch, ch, cm, cm, cl], 32).astype(BF16),
            pad_rows([eh, em, el, eh, em, eh], 32).astype(BF16),
            TN,
        )
        stacked = pad_rows(errors, 16).astype(BF16)
        dcol = dot(stacked, wh, NT) + dot(stacked, wl, NT)
        dcol = dcol[0:3] + dcol[3:6] + dcol[6:9]

        h_ref[...] = dw * w_ref[...]
        run = jnp.zeros((8, PIX), F32)
        for v in range(steps):
            run = run + h_ref[8 * v : 8 * v + 8, :]
        behind = scan_rows(run, None, 0.0, False, lambda u, w: u + w)
        for v in reversed(range(steps)):
            alpha = alpha_ref[8 * v : 8 * v + 8, :]
            u = h_ref[8 * v : 8 * v + 8, :]
            h_ref[8 * v : 8 * v + 8, :] = u - behind * (alpha / (1.0 - alpha))
            behind = behind + u

        h = h_ref[...]

        def moment(z):
            zh, zl = split(z, 2)
            return dot(moments, zh, NT) + dot(moments, zl, NT)

        m0, m1, m2 = moment(h), moment(-h * f1_ref[...]), moment(-h * f2_ref[...])
        s1, s2 = m1[0:1], m2[0:1]
        grads = pad_rows(
            [
                -a * s1,
                -b * s1 - c2 * s2,
                m1[1:2] - mx * s1,
                m1[2:3] - my * s1,
                m2[2:3] - my * s2,
                unsig * m0[0:1],
                dcol,
            ],
            ROWS,
        )
        sent = jnp.concatenate([jnp.where(own == c, grads, 0.0) for c in range(cells)], axis=0)
        sent = jnp.concatenate(split(sent, 3), axis=1)
        put = dot(sent, jnp.concatenate([place, place, place], axis=1), NT)
        out_ref[...] += put.reshape(out_ref.shape)
        return carry

    lax.fori_loop(0, tiles, tile, 0)


def collect(incoming_ref, rows_ref, grad_ref, total_ref):
    cells, _, cap = incoming_ref.shape
    groups = grad_ref.shape[1] // LANES
    total_ref[...] = jnp.zeros_like(total_ref)

    def cell(c, carry):
        row = rows_ref[pl.ds(c, 1), :]
        low = one_hot(row & (LANES - 1), LANES).astype(BF16)
        high = row // LANES
        part = incoming_ref[pl.ds(c, 1)][0]
        placed = jnp.concatenate([jnp.where(high == g, part, 0.0) for g in range(groups)], axis=0)
        placed = jnp.concatenate(split(placed, 3), axis=1)
        total_ref[...] += dot(placed, jnp.concatenate([low, low, low], axis=1), NT)
        return carry

    lax.fori_loop(0, cells, cell, 0)
    for g in range(groups):
        grad_ref[:, g * LANES : (g + 1) * LANES] = total_ref[g * ROWS : g * ROWS + PARAMS, :]


def call(body, out, scratch):
    return pl.pallas_call(
        body,
        out_shape=out,
        scratch_shapes=scratch,
        compiler_params=pltpu.CompilerParams(vmem_limit_bytes=48 * 1024 * 1024),
    )


def per_device(splats, target, slot_owner, slot_row, depth_order, tile_count):
    cells = lax.axis_size("cell")
    owned = splats.shape[1]
    tiles, block = slot_row.shape
    cap = max(2, 2 * tiles * block // cells)
    order = depth_order.reshape(tiles, 8, block // 8).transpose(0, 2, 1).reshape(tiles, block)
    owner = slot_owner.reshape(tiles, block)
    shape = jax.ShapeDtypeStruct
    own, pos, asking = call(
        plan_slots,
        (shape((tiles, block), I32), shape((tiles, block), I32), shape((cells, cap), I32)),
        [pltpu.VMEM((2 * cells, cap), F32)],
    )(order, owner, slot_row)
    received = lax.all_to_all(asking, "cell", split_axis=0, concat_axis=0, tiled=True)
    values = call(answer, shape((cells, ROWS, cap), F32), [])(splats, received)
    values = lax.all_to_all(values, "cell", split_axis=0, concat_axis=0, tiled=True)
    rendered, outgoing = call(
        shade,
        (shape(target.shape, F32), shape((cells, ROWS, cap), F32)),
        [pltpu.VMEM((cells * ROWS, 3 * cap), BF16)] + [pltpu.VMEM((block, PIX), F32)] * 5,
    )(values, own, pos, order, tile_count.reshape(tiles, 1), target)
    incoming = lax.all_to_all(outgoing, "cell", split_axis=0, concat_axis=0, tiled=True)
    grad_splats = call(
        collect, shape((PARAMS, owned), F32), [pltpu.VMEM((owned // LANES * ROWS, LANES), F32)]
    )(incoming, received)
    return (rendered, grad_splats)


def solution(mesh):
    in_specs = (
        P(None, "cell"),
        P(None, "cell"),
        P("cell", None, None),
        P("cell", None),
        P("cell", None),
        P("cell"),
    )
    out_specs = (P(None, "cell"), P(None, "cell"))
    return jax.shard_map(
        per_device, mesh=mesh, in_specs=in_specs, out_specs=out_specs, check_vma=False
    )
```

time: 708 us -> 116 us (0.16)
  the two profiles are of different devices: /device:TPU:13 before, /device:TPU:0 now
where the time goes in v1:
time: 116 us
  Pallas kernels  62.6 us (54%)
  blocking collectives  32.7 us (28%)
  waiting for transfers between devices  14.8 us (13%)
  starting transfers between devices  2.73 us (2%)
  local copies, waits for them, and re-layouts  2.42 us (2%)
    pallas_call x1, Pallas kernels, per_device(): call(shade, (shape(target.shape, F32), shape((cells, ROWS, cap), F32)), [...  36.9 us
    all_to_all x1, blocking collectives, per_device(): lax.all_to_all(outgoing, 'cell', split_axis=0, concat_axis=0, tiled=True)  18.3 us
    all_to_all x1, waiting for transfers between devices, per_device(): lax.all_to_all(values, 'cell', split_axis=0, concat_axis=0, tiled=True)  14.8 us
    all_to_all x1, blocking collectives, per_device(): lax.all_to_all(asking, 'cell', split_axis=0, concat_axis=0, tiled=True)  14.4 us
    pallas_call x1, Pallas kernels, per_device(): call(collect, shape((PARAMS, owned), F32), [pltpu.VMEM((owned // LANES *...  9.84 us
    pallas_call x1, Pallas kernels, per_device(): values = call(answer, shape((cells, ROWS, cap), F32), [])(splats, received)  8.11 us
    pallas_call x1, Pallas kernels, per_device(): call(plan_slots, (shape((tiles, block), I32), shape((tiles, block), I32),...  7.77 us
    all_to_all x1, starting transfers between devices, per_device(): lax.all_to_all(values, 'cell', split_axis=0, concat_axis=0, tiled=True)  2.73 us
  transfers between devices with their start and end apart: 1, of which 1 were waited for; matrix products, arithmetic and copies ran while one was open for 0% of the time, Pallas kernels for 0%

profile of v1, /device:TPU:0, one launch (start us, length us, event | category | flops | bytes accessed | tf_op | source)
XLA Modules:
  0.0 115.9 jit_solution(2811186294327191194)
XLA Ops:
  0.6 0.0 copy-start.3
  0.6 0.7 copy.24
  1.4 0.0 copy-done.3
  1.4 0.1 reshape.18
  1.4 0.1 copy.14
  1.6 0.0 copy-start.2
  1.6 0.1 copy.15.order_ref
  1.6 0.0 copy-start
  1.6 0.6 copy-done.2
  2.3 7.8 %shard_map.77 = (s32[16,256]{1,0:T(8,128)S(1)}, s32[16,256]{1,0:T(8,128)S(1)}, s32[32,256]{1,0:T(8,128)S(1)}) custom-call(s32[16,256]{1,0:T(8,128)S(1)} %copy.15.order_ref, s32[16,256]{1,0:T(8,128)S(1)} %bitcast.13, s32[16,256]{1,0:T(8,128)S(1)} %copy-done.2), custom_call_target="tpu_custom_call" | custom-call | tf_op jit(solution)/shard_map/pallas_call | solution.py:268
  10.1 14.4 %all_to_all.21 = s32[32,1,256]{2,1,0:T(1,128)S(1)} all-to-all(s32[32,1,256]{2,1,0:T(1,128)S(1)} %copy.16), channel_id=1, replica_groups=mesh['cell'=32] {'cell'}, dimensions={0} | all-to-all | bytes 65536 | tf_op jit(solution)/shard_map/all_to_all | solution.py:273
  24.5 0.0 copy-done
  24.5 8.1 %shard_map.78 = f32[32,16,256]{2,1,0:T(8,128)} custom-call(f32[9,2048]{1,0:T(8,128)S(1)} %copy-done, s32[32,256]{1,0:T(8,128)S(1)} %bitcast.11), custom_call_target="tpu_custom_call" | custom-call | tf_op jit(solution)/shard_map/pallas_call | solution.py:274
  32.6 0.0 copy-start.1
  32.6 2.7 %all-to-all-start.1 = ((f32[32,16,256]{2,1,0:T(8,128)}), f32[32,16,256]{2,1,0:T(8,128)S(1)}, u32[]{:S(2)}, u32[]{:S(2)}) async-start(f32[32,16,256]{2,1,0:T(8,128)} %shard_map.78), calls=%async_computation.1 | async-start | bytes 1048576 | tf_op jit(solution)/shard_map/all_to_all | solution.py:275
  35.3 0.0 copy-start.4
  35.3 0.6 copy-done.4
  36.0 0.1 copy.18.count_ref
  36.1 14.8 %all-to-all-done.1.values_ref = f32[32,16,256]{2,1,0:T(8,128)S(1)} async-done(((f32[32,16,256]{2,1,0:T(8,128)}), f32[32,16,256]{2,1,0:T(8,128)S(1)}, u32[]{:S(2)}, u32[]{:S(2)}) %all-to-all-start.1) | async-done | bytes 524320 | tf_op jit(solution)/shard_map/all_to_all | solution.py:275
  50.9 0.0 copy-done.1
  50.9 36.9 %shard_map.79 = (f32[3,4096]{1,0:T(4,128)}, f32[32,16,256]{2,1,0:T(8,128)S(1)}) custom-call(f32[32,16,256]{2,1,0:T(8,128)S(1)} %all-to-all-done.1.values_ref, s32[16,256]{1,0:T(8,128)S(1)} %get-tuple-element.8.own_ref, s32[16,256]{1,0:T(8,128)S(1)} %get-tuple-element.9.pos_ref, s32[16,256]{1,0:T(8,128)S(1)} %copy.15.order_ref, s32[16,1]{1,0:T(8,128)S(1)} %copy.18.count_ref, ...), custom_call_target="tpu_custom_call" | custom-call | tf_op jit(solution)/shard_map/pallas_call | solution.py:276
  87.8 18.3 %all_to_all.22.incoming_ref = f32[32,16,256]{2,1,0:T(8,128)S(1)} all-to-all(f32[32,16,256]{2,1,0:T(8,128)S(1)} %get-tuple-element.11), channel_id=1, replica_groups=mesh['cell'=32] {'cell'}, dimensions={0} | all-to-all | bytes 1048576 | tf_op jit(solution)/shard_map/all_to_all | solution.py:281
  106.1 9.8 %shard_map.80 = f32[9,2048]{1,0:T(8,128)} custom-call(f32[32,16,256]{2,1,0:T(8,128)S(1)} %all_to_all.22.incoming_ref, s32[32,256]{1,0:T(8,128)S(1)} %bitcast.12), custom_call_target="tpu_custom_call" | custom-call | tf_op jit(solution)/shard_map/pallas_call | solution.py:282
  (2 shorter events, 0.0 us)
Async XLA Ops:
  0.6 0.7 copy-start.3
  1.6 0.7 copy-start.2
  1.6 22.8 %copy-start = (f32[9,2048]{1,0:T(8,128)S(1)}, f32[9,2048]{1,0:T(8,128)}, u32[]{:S(2)}) copy-start(f32[9,2048]{1,0:T(8,128)} %splats_ref.1) | copy-start | bytes 221188
  32.6 18.3 %copy-start.1 = (f32[3,4096]{1,0:T(4,128)S(1)}, f32[3,4096]{1,0:T(4,128)}, u32[]{:S(2)}) copy-start(f32[3,4096]{1,0:T(4,128)} %target_ref.1) | copy-start | bytes 147460
  32.6 18.3 %all-to-all-start.1 = ((f32[32,16,256]{2,1,0:T(8,128)}), f32[32,16,256]{2,1,0:T(8,128)S(1)}, u32[]{:S(2)}, u32[]{:S(2)}) async-start(f32[32,16,256]{2,1,0:T(8,128)} %shard_map.78), calls=%async_computation.1 | async-start | bytes 1048576 | tf_op jit(solution)/shard_map/all_to_all | solution.py:275
  35.3 0.7 copy-start.4

commit v2 on v1

--- a/solution.py
+++ b/solution.py
@@ -1,5 +1,3 @@
-import functools
-
 import jax
 import jax.numpy as jnp
 from jax import lax
@@ -47,7 +45,7 @@
 
 def plan_slots(order_ref, owner_ref, row_ref, own_ref, pos_ref, ask_ref, parts_ref):
     tiles, block = order_ref.shape
-    cells, cap = ask_ref.shape
+    cells, _, cap = ask_ref.shape
     before = jnp.where(iota((block, block), 0) < iota((block, block), 1), 1.0, 0.0).astype(BF16)
     parts_ref[...] = jnp.zeros_like(parts_ref)
 
@@ -71,29 +69,28 @@
 
     lax.fori_loop(0, tiles, tile, jnp.zeros((cells, 1), F32))
     both = parts_ref[...].astype(I32)
-    ask_ref[...] = both[:cells] * 256 + both[cells:]
-
-
-def answer(splats_ref, rows_ref, values_ref):
-    cells, cap = rows_ref.shape
+    both = both[:cells] * 256 + both[cells:]
+    for c in range(cells):
+        ask_ref[c] = both[c : c + 1]
+
+
+def splat_table(splats_ref):
     groups = splats_ref.shape[1] // LANES
     table = jnp.concatenate(
         [pad_rows([splats_ref[:, g * LANES : (g + 1) * LANES]], ROWS) for g in range(groups)], axis=0
     )
-    table = jnp.concatenate(split(table, 3), axis=1)
-
-    def cell(c, carry):
-        row = rows_ref[pl.ds(c, 1), :]
-        low = one_hot(row & (LANES - 1), LANES).astype(BF16)
-        found = dot(table, jnp.concatenate([low, low, low], axis=0))
-        high = row // LANES
-        total = jnp.zeros((ROWS, cap), F32)
-        for g in range(groups):
-            total += jnp.where(high == g, found[g * ROWS : (g + 1) * ROWS], 0.0)
-        values_ref[pl.ds(c, 1)] = total[None]
-        return carry
-
-    lax.fori_loop(0, cells, cell, 0)
+    return jnp.concatenate(split(table, 3), axis=1)
+
+
+def answer(lookup_ref, row):
+    groups = lookup_ref.shape[0] // ROWS
+    low = one_hot(row & (LANES - 1), LANES).astype(BF16)
+    found = dot(lookup_ref[...], jnp.concatenate([low, low, low], axis=0))
+    high = row // LANES
+    total = jnp.zeros((ROWS, row.shape[1]), F32)
+    for g in range(groups):
+        total += jnp.where(high == g, found[g * ROWS : (g + 1) * ROWS], 0.0)
+    return total[:PARAMS]
 
 
 def scan_rows(x, keep, fill, down, combine):
@@ -112,7 +109,7 @@
 
 def shade(
     values_ref, own_ref, pos_ref, order_ref, count_ref, target_ref, rendered_ref, out_ref,
-    table_ref, f1_ref, f2_ref, alpha_ref, w_ref, h_ref,
+    total_ref, table_ref, f1_ref, f2_ref, alpha_ref, w_ref, h_ref,
 ):
     tiles, block = own_ref.shape
     cells, _, cap = values_ref.shape
@@ -133,9 +130,9 @@
     moments = pad_rows([one, x, y], 16).astype(BF16)
 
     for c in range(cells):
-        for part, piece in enumerate(split(values_ref[c], 3)):
+        for part, piece in enumerate(split(pad_rows([values_ref[c]], ROWS), 3)):
             table_ref[c * ROWS : (c + 1) * ROWS, part * cap : (part + 1) * cap] = piece
-    out_ref[...] = jnp.zeros_like(out_ref)
+    total_ref[...] = jnp.zeros_like(total_ref)
 
     def tile(t, carry):
         at = pl.ds(t, 1)
@@ -221,40 +218,94 @@
         )
         sent = jnp.concatenate([jnp.where(own == c, grads, 0.0) for c in range(cells)], axis=0)
         sent = jnp.concatenate(split(sent, 3), axis=1)
-        put = dot(sent, jnp.concatenate([place, place, place], axis=1), NT)
-        out_ref[...] += put.reshape(out_ref.shape)
+        total_ref[...] += dot(sent, jnp.concatenate([place, place, place], axis=1), NT)
         return carry
 
     lax.fori_loop(0, tiles, tile, 0)
-
-
-def collect(incoming_ref, rows_ref, grad_ref, total_ref):
-    cells, _, cap = incoming_ref.shape
-    groups = grad_ref.shape[1] // LANES
-    total_ref[...] = jnp.zeros_like(total_ref)
-
-    def cell(c, carry):
-        row = rows_ref[pl.ds(c, 1), :]
-        low = one_hot(row & (LANES - 1), LANES).astype(BF16)
-        high = row // LANES
-        part = incoming_ref[pl.ds(c, 1)][0]
-        placed = jnp.concatenate([jnp.where(high == g, part, 0.0) for g in range(groups)], axis=0)
-        placed = jnp.concatenate(split(placed, 3), axis=1)
-        total_ref[...] += dot(placed, jnp.concatenate([low, low, low], axis=1), NT)
+    for c in range(cells):
+        out_ref[c] = total_ref[c * ROWS : c * ROWS + PARAMS, :]
+
+
+def collect(part, row, total_ref):
+    groups = total_ref.shape[0] // ROWS
+    low = one_hot(row & (LANES - 1), LANES).astype(BF16)
+    high = row // LANES
+    part = pad_rows([part], ROWS)
+    placed = jnp.concatenate([jnp.where(high == g, part, 0.0) for g in range(groups)], axis=0)
+    placed = jnp.concatenate(split(placed, 3), axis=1)
+    total_ref[...] += dot(placed, jnp.concatenate([low, low, low], axis=1), NT)
+
+
+def splatting(
+    splats_ref, order_ref, owner_ref, row_ref, count_ref, target_ref, rendered_ref, grad_ref,
+    own_ref, pos_ref, ask_ref, asked_ref, reply_ref, values_ref, out_ref, incoming_ref,
+    parts_ref, lookup_ref, sums_ref, shade_refs, send_sem, recv_sem,
+):
+    cells = ask_ref.shape[0]
+    me = lax.axis_index("cell")
+    barrier = pltpu.get_barrier_semaphore()
+
+    def greet(step, carry):
+        pl.semaphore_signal(
+            barrier, inc=1, device_id=(lax.rem(me + step, cells),), device_id_type=pl.DeviceIdType.MESH
+        )
         return carry
 
-    lax.fori_loop(0, cells, cell, 0)
-    for g in range(groups):
-        grad_ref[:, g * LANES : (g + 1) * LANES] = total_ref[g * ROWS : g * ROWS + PARAMS, :]
-
-
-def call(body, out, scratch):
-    return pl.pallas_call(
-        body,
-        out_shape=out,
-        scratch_shapes=scratch,
-        compiler_params=pltpu.CompilerParams(vmem_limit_bytes=48 * 1024 * 1024),
-    )
+    def over_others(body):
+        def one(step, carry):
+            body(lax.rem(me + step, cells), lax.rem(me + cells - step, cells))
+            return carry
+
+        lax.fori_loop(1, cells, one, 0)
+
+    def copy(phase, source_ref, landing_ref, to, slot):
+        return pltpu.make_async_remote_copy(
+            src_ref=source_ref.at[to],
+            dst_ref=landing_ref.at[slot],
+            send_sem=send_sem.at[phase, to],
+            recv_sem=recv_sem.at[phase, slot],
+            device_id=(to,),
+            device_id_type=pl.DeviceIdType.MESH,
+        )
+
+    lax.fori_loop(1, cells, greet, 0)
+    plan_slots(order_ref, owner_ref, row_ref, own_ref, pos_ref, ask_ref, parts_ref)
+    pl.semaphore_wait(barrier, cells - 1)
+    over_others(lambda to, source: copy(0, ask_ref, asked_ref, to, me).start())
+
+    lookup_ref[...] = splat_table(splats_ref)
+    asked_ref[me] = ask_ref[me]
+    values_ref[me] = answer(lookup_ref, asked_ref[me])
+
+    def serve(to, source):
+        copy(0, ask_ref, asked_ref, source, source).wait_recv()
+        reply_ref[source] = answer(lookup_ref, asked_ref[source])
+        copy(1, reply_ref, values_ref, source, me).start()
+
+    over_others(serve)
+    over_others(lambda to, source: copy(1, reply_ref, values_ref, to, to).wait_recv())
+    shade(
+        values_ref, own_ref, pos_ref, order_ref, count_ref, target_ref, rendered_ref, out_ref,
+        *shade_refs,
+    )
+    over_others(lambda to, source: copy(2, out_ref, incoming_ref, to, me).start())
+    sums_ref[...] = jnp.zeros_like(sums_ref)
+    collect(out_ref[me], asked_ref[me], sums_ref)
+
+    def receive(to, source):
+        copy(2, out_ref, incoming_ref, source, source).wait_recv()
+        collect(incoming_ref[source], asked_ref[source], sums_ref)
+
+    over_others(receive)
+    for g in range(grad_ref.shape[1] // LANES):
+        grad_ref[:, g * LANES : (g + 1) * LANES] = sums_ref[g * ROWS : g * ROWS + PARAMS, :]
+
+    def finish(to, source):
+        copy(0, ask_ref, asked_ref, to, me).wait_send()
+        copy(1, reply_ref, values_ref, to, me).wait_send()
+        copy(2, out_ref, incoming_ref, to, me).wait_send()
+
+    over_others(finish)
 
 
 def per_device(splats, target, slot_owner, slot_row, depth_order, tile_count):
@@ -264,25 +315,37 @@
     cap = max(2, 2 * tiles * block // cells)
     order = depth_order.reshape(tiles, 8, block // 8).transpose(0, 2, 1).reshape(tiles, block)
     owner = slot_owner.reshape(tiles, block)
-    shape = jax.ShapeDtypeStruct
-    own, pos, asking = call(
-        plan_slots,
-        (shape((tiles, block), I32), shape((tiles, block), I32), shape((cells, cap), I32)),
-        [pltpu.VMEM((2 * cells, cap), F32)],
-    )(order, owner, slot_row)
-    received = lax.all_to_all(asking, "cell", split_axis=0, concat_axis=0, tiled=True)
-    values = call(answer, shape((cells, ROWS, cap), F32), [])(splats, received)
-    values = lax.all_to_all(values, "cell", split_axis=0, concat_axis=0, tiled=True)
-    rendered, outgoing = call(
-        shade,
-        (shape(target.shape, F32), shape((cells, ROWS, cap), F32)),
-        [pltpu.VMEM((cells * ROWS, 3 * cap), BF16)] + [pltpu.VMEM((block, PIX), F32)] * 5,
-    )(values, own, pos, order, tile_count.reshape(tiles, 1), target)
-    incoming = lax.all_to_all(outgoing, "cell", split_axis=0, concat_axis=0, tiled=True)
-    grad_splats = call(
-        collect, shape((PARAMS, owned), F32), [pltpu.VMEM((owned // LANES * ROWS, LANES), F32)]
-    )(incoming, received)
-    return (rendered, grad_splats)
+    grouped = owned // LANES * ROWS
+    vmem = pltpu.VMEM
+    return pl.pallas_call(
+        splatting,
+        out_shape=(
+            jax.ShapeDtypeStruct(target.shape, F32),
+            jax.ShapeDtypeStruct((PARAMS, owned), F32),
+        ),
+        in_specs=[pl.BlockSpec(memory_space=pltpu.VMEM)] * 6,
+        out_specs=[pl.BlockSpec(memory_space=pltpu.VMEM)] * 2,
+        scratch_shapes=[
+            vmem((tiles, block), I32),
+            vmem((tiles, block), I32),
+            vmem((cells, 1, cap), I32),
+            vmem((cells, 1, cap), I32),
+            vmem((cells, PARAMS, cap), F32),
+            vmem((cells, PARAMS, cap), F32),
+            vmem((cells, PARAMS, cap), F32),
+            vmem((cells, PARAMS, cap), F32),
+            vmem((2 * cells, cap), F32),
+            vmem((grouped, 3 * LANES), BF16),
+            vmem((grouped, LANES), F32),
+            [vmem((cells * ROWS, cap), F32), vmem((cells * ROWS, 3 * cap), BF16)]
+            + [vmem((block, PIX), F32)] * 5,
+            pltpu.SemaphoreType.DMA((3, cells)),
+            pltpu.SemaphoreType.DMA((3, cells)),
+        ],
+        compiler_params=pltpu.CompilerParams(
+            vmem_limit_bytes=48 * 1024 * 1024, collective_id=0, has_side_effects=True
+        ),
+    )(splats, order, owner, slot_row, tile_count.reshape(tiles, 1), target)
 
 
 def solution(mesh):

time: 116 us -> 86 us (0.74)
  the two profiles are of different devices: /device:TPU:0 before, /device:TPU:25 now
where the time goes in v2:
time: 86 us; the launch traced here: 85.7 us
  Pallas kernels  81.2 us (94%)
  local copies, waits for them, and re-layouts  3.79 us (4%)
    pallas_call x1, Pallas kernels, per_device(): pl.pallas_call(splatting, out_shape=(jax.ShapeDtypeStruct(target.shape, F...  81.2 us
    unnamed x13, local copies, waits for them, and re-layouts  3.46 us

profile of v2, /device:TPU:25, one launch (start us, length us, event | category | flops | bytes accessed | tf_op | source)
XLA Modules:
  0.0 85.7 jit_solution(6094608347841305017)
XLA Ops:
  0.6 0.0 copy-start.4
  0.6 0.6 copy-done.4
  1.3 0.1 copy.12.count_ref
  1.4 0.0 copy-start.3
  1.4 0.7 copy.15
  2.1 0.0 copy-done.3
  2.1 0.1 reshape.16
  2.2 0.0 copy-start
  2.2 0.1 copy.10
  2.3 0.0 copy-start.1
  2.3 0.0 copy-start.2
  2.3 0.1 copy.11.order_ref
  2.4 0.7 copy-done
  3.1 0.1 copy-done.1
  3.2 0.0 copy-done.2
  3.2 81.2 %shard_map.77 = (f32[3,4096]{1,0:T(4,128)S(1)}, f32[9,2048]{1,0:T(8,128)S(1)}) custom-call(f32[9,2048]{1,0:T(8,128)S(1)} %copy-done, s32[16,256]{1,0:T(8,128)S(1)} %copy.11.order_ref, s32[16,256]{1,0:T(8,128)S(1)} %bitcast.7, s32[16,256]{1,0:T(8,128)S(1)} %copy-done.2, s32[16,1]{1,0:T(8,128)S(1)} %copy.12.count_ref, f32[3,4096]{1,0:T(4,128)S(1)} %copy-done.1), custom_call_target="tpu_custom_call" | custom-call | tf_op jit(solution)/shard_map/pallas_call | solution.py:320
  84.4 0.6 copy.18
  85.0 0.7 copy.19
Async XLA Ops:
  0.6 0.7 copy-start.4
  1.4 0.7 copy-start.3
  2.2 0.9 %copy-start = (f32[9,2048]{1,0:T(8,128)S(1)}, f32[9,2048]{1,0:T(8,128)}, u32[]{:S(2)}) copy-start(f32[9,2048]{1,0:T(8,128)} %splats_ref.1) | copy-start | bytes 221188
  2.3 0.9 %copy-start.1 = (f32[3,4096]{1,0:T(4,128)S(1)}, f32[3,4096]{1,0:T(4,128)}, u32[]{:S(2)}) copy-start(f32[3,4096]{1,0:T(4,128)} %target_ref.1) | copy-start | bytes 147460
  2.3 0.8 copy-start.2

commit v3 on v2

--- a/solution.py
+++ b/solution.py
@@ -7,7 +7,6 @@
 
 SIDE = 16
 PIX = SIDE * SIDE
-ROWS = 16
 PARAMS = 9
 LANES = 128
 F32, BF16, I32 = jnp.float32, jnp.bfloat16, jnp.int32
@@ -43,13 +42,45 @@
     return jnp.concatenate(pieces, axis=0)
 
 
+def lockstep(works):
+    works = list(works)
+    while works:
+        works = [work for work in works if next(work, "end") is None]
+
+
+def group_of(count):
+    return next(size for size in (4, 2, 1) if count % size == 0)
+
+
+def gather(table, place, mask):
+    found = dot(table, jnp.concatenate([place, place, place], axis=0))
+    high = mask.shape[0]
+    return [
+        jnp.sum(found[c * high : (c + 1) * high] * mask, axis=0, keepdims=True) for c in range(PARAMS)
+    ]
+
+
+def scatter(rows, place, mask):
+    mask = mask.astype(BF16)
+    pieces = split(rows, 2)
+    spread = jnp.concatenate(
+        [
+            jnp.concatenate([piece[c : c + 1] * mask for c in range(PARAMS)], axis=0)
+            for piece in pieces
+        ],
+        axis=1,
+    )
+    return dot(spread, jnp.concatenate([place, place], axis=1), NT)
+
+
 def plan_slots(order_ref, owner_ref, row_ref, own_ref, pos_ref, ask_ref, parts_ref):
     tiles, block = order_ref.shape
     cells, _, cap = ask_ref.shape
     before = jnp.where(iota((block, block), 0) < iota((block, block), 1), 1.0, 0.0).astype(BF16)
     parts_ref[...] = jnp.zeros_like(parts_ref)
-
-    def tile(t, seen):
+    group = group_of(tiles)
+
+    def tile(t, state, asks):
         at = pl.ds(t, 1)
         chosen = one_hot(order_ref[at, :], block).astype(BF16)
         row = row_ref[at, :]
@@ -57,40 +88,45 @@
             [owner_ref[at, :].astype(F32), (row >> 8).astype(F32), (row & 255).astype(F32)], 16
         )
         moved = dot(source.astype(BF16), chosen)
+        yield
         own = moved[0:1].astype(I32)
+        own_ref[at, :] = own
         mine = one_hot(own, cells)
-        earlier = dot(mine.astype(BF16), before) + seen
+        within = dot(mine.astype(BF16), before)
+        asked = jnp.concatenate([mine * moved[1:2], mine * moved[2:3]], axis=0).astype(BF16)
+        earlier = within + state[0]
+        state[0] = state[0] + jnp.sum(mine, axis=1, keepdims=True)
+        yield
         pos = jnp.sum(mine * earlier, axis=0, keepdims=True).astype(I32)
-        own_ref[at, :] = own
         pos_ref[at, :] = pos
-        asked = jnp.concatenate([mine * moved[1:2], mine * moved[2:3]], axis=0).astype(BF16)
-        parts_ref[...] += dot(asked, one_hot(pos, cap).astype(BF16), NT)
-        return seen + jnp.sum(mine, axis=1, keepdims=True)
-
-    lax.fori_loop(0, tiles, tile, jnp.zeros((cells, 1), F32))
+        asks.append(dot(asked, one_hot(pos, cap).astype(BF16), NT))
+
+    def some(i, seen):
+        state, asks = [seen], []
+        lockstep(tile(i * group + j, state, asks) for j in range(group))
+        parts_ref[...] += sum(asks[1:], asks[0])
+        return state[0]
+
+    lax.fori_loop(0, tiles // group, some, jnp.zeros((cells, 1), F32))
     both = parts_ref[...].astype(I32)
     both = both[:cells] * 256 + both[cells:]
     for c in range(cells):
         ask_ref[c] = both[c : c + 1]
 
 
-def splat_table(splats_ref):
+def splat_table(splats_ref, rows_ref):
     groups = splats_ref.shape[1] // LANES
-    table = jnp.concatenate(
-        [pad_rows([splats_ref[:, g * LANES : (g + 1) * LANES]], ROWS) for g in range(groups)], axis=0
-    )
-    return jnp.concatenate(split(table, 3), axis=1)
+    for c in range(PARAMS):
+        for g in range(groups):
+            at = c * groups + g
+            rows_ref[at : at + 1, :] = splats_ref[c : c + 1, g * LANES : (g + 1) * LANES]
+    return jnp.concatenate(split(rows_ref[...], 3), axis=1)
 
 
 def answer(lookup_ref, row):
-    groups = lookup_ref.shape[0] // ROWS
     low = one_hot(row & (LANES - 1), LANES).astype(BF16)
-    found = dot(lookup_ref[...], jnp.concatenate([low, low, low], axis=0))
-    high = row // LANES
-    total = jnp.zeros((ROWS, row.shape[1]), F32)
-    for g in range(groups):
-        total += jnp.where(high == g, found[g * ROWS : (g + 1) * ROWS], 0.0)
-    return total[:PARAMS]
+    mask = one_hot(row >> 7, lookup_ref.shape[0] // PARAMS)
+    return jnp.concatenate(gather(lookup_ref[...], low, mask), axis=0)
 
 
 def scan_rows(x, keep, fill, down, combine):
@@ -109,7 +145,7 @@
 
 def shade(
     values_ref, own_ref, pos_ref, order_ref, count_ref, target_ref, rendered_ref, out_ref,
-    total_ref, table_ref, f1_ref, f2_ref, alpha_ref, w_ref, h_ref,
+    total_ref, table_ref, tile_refs,
 ):
     tiles, block = own_ref.shape
     cells, _, cap = values_ref.shape
@@ -129,33 +165,35 @@
     linear = pad_rows([linear, linear, linear], 32).astype(BF16)
     moments = pad_rows([one, x, y], 16).astype(BF16)
 
-    for c in range(cells):
-        for part, piece in enumerate(split(pad_rows([values_ref[c]], ROWS), 3)):
-            table_ref[c * ROWS : (c + 1) * ROWS, part * cap : (part + 1) * cap] = piece
+    for c in range(PARAMS):
+        for part, piece in enumerate(split(values_ref[:, c, :], 3)):
+            table_ref[c * cells : (c + 1) * cells, part * cap : (part + 1) * cap] = piece
     total_ref[...] = jnp.zeros_like(total_ref)
 
-    def tile(t, carry):
+    def tile(t, refs, puts):
+        f1_ref, f2_ref, alpha_ref, w_ref, h_ref = refs
         at = pl.ds(t, 1)
         own = own_ref[at, :]
         place = one_hot(pos_ref[at, :], cap).astype(BF16)
-        found = dot(table_ref[...], jnp.concatenate([place, place, place], axis=0))
-        p = jnp.zeros((ROWS, block), F32)
-        for c in range(cells):
-            p += jnp.where(own == c, found[c * ROWS : (c + 1) * ROWS], 0.0)
+        mine = one_hot(own, cells)
+        p = gather(table_ref[...], place, mine)
+        yield
         live = jnp.where(order_ref[at, :] < count_ref[at, :], 1.0, 0.0)
-        mx, my = p[0:1] - SIDE / 2, p[1:2] - SIDE / 2
-        a, b, c2 = p[2:3], p[3:4], p[4:5]
-        colour = p[6:9]
-        sig = 1.0 / (1.0 + jnp.exp(-p[5:6]))
-        unsig = 1.0 / (1.0 + jnp.exp(p[5:6]))
+        mx, my = p[0] - SIDE / 2, p[1] - SIDE / 2
+        a, b, c2 = p[2], p[3], p[4]
+        colour = jnp.concatenate(p[6:9], axis=0)
+        sig = 1.0 / (1.0 + jnp.exp(-p[5]))
+        unsig = 1.0 / (1.0 + jnp.exp(p[5]))
         factors = pad_rows([a, b, -(a * mx + b * my), c2, -(c2 * my), sig * live], 8)
         factors = pad_rows([z.astype(F32) for z in split(factors, 3)], 32).astype(BF16)
         spread = dot(factors, linear, TN)
+        yield
         f1, f2 = spread[:, :PIX], spread[:, PIX : 2 * PIX]
         f1_ref[...] = f1
         f2_ref[...] = f2
         alpha_ref[...] = spread[:, 2 * PIX :] * jnp.exp(-0.5 * (f1 * f1 + f2 * f2))
 
+        yield
         run = jnp.ones((8, PIX), F32)
         for v in range(steps):
             alpha = alpha_ref[8 * v : 8 * v + 8, :]
@@ -165,11 +203,13 @@
         for v in range(steps):
             w_ref[8 * v : 8 * v + 8, :] *= ahead
 
+        yield
         colours = [z.astype(F32) for z in split(colour, 3)]
         ch, cm, cl = colours
         wh, wl = split(w_ref[...], 2)
         stacked = pad_rows(colours, 16).astype(BF16)
         picture = dot(stacked, wh) + dot(stacked, wl)
+        yield
         picture = picture[0:3] + picture[3:6] + picture[6:9]
         lanes = pl.ds(pl.multiple_of(t * PIX, PIX), PIX)
         rendered_ref[:, lanes] = picture
@@ -183,6 +223,7 @@
         )
         stacked = pad_rows(errors, 16).astype(BF16)
         dcol = dot(stacked, wh, NT) + dot(stacked, wl, NT)
+        yield
         dcol = dcol[0:3] + dcol[3:6] + dcol[6:9]
 
         h_ref[...] = dw * w_ref[...]
@@ -196,6 +237,7 @@
             h_ref[8 * v : 8 * v + 8, :] = u - behind * (alpha / (1.0 - alpha))
             behind = behind + u
 
+        yield
         h = h_ref[...]
 
         def moment(z):
@@ -203,6 +245,7 @@
             return dot(moments, zh, NT) + dot(moments, zl, NT)
 
         m0, m1, m2 = moment(h), moment(-h * f1_ref[...]), moment(-h * f2_ref[...])
+        yield
         s1, s2 = m1[0:1], m2[0:1]
         grads = pad_rows(
             [
@@ -214,26 +257,26 @@
                 unsig * m0[0:1],
                 dcol,
             ],
-            ROWS,
+            PARAMS,
         )
-        sent = jnp.concatenate([jnp.where(own == c, grads, 0.0) for c in range(cells)], axis=0)
-        sent = jnp.concatenate(split(sent, 3), axis=1)
-        total_ref[...] += dot(sent, jnp.concatenate([place, place, place], axis=1), NT)
+        puts.append(scatter(grads, place, mine))
+
+    group = len(tile_refs)
+
+    def some(i, carry):
+        puts = []
+        lockstep(tile(i * group + j, tile_refs[j], puts) for j in range(group))
+        total_ref[...] += sum(puts[1:], puts[0])
         return carry
 
-    lax.fori_loop(0, tiles, tile, 0)
-    for c in range(cells):
-        out_ref[c] = total_ref[c * ROWS : c * ROWS + PARAMS, :]
-
-
-def collect(part, row, total_ref):
-    groups = total_ref.shape[0] // ROWS
+    lax.fori_loop(0, tiles // group, some, 0)
+    for c in range(PARAMS):
+        out_ref[:, c, :] = total_ref[c * cells : (c + 1) * cells, :]
+
+
+def collect(part, row, groups):
     low = one_hot(row & (LANES - 1), LANES).astype(BF16)
-    high = row // LANES
-    part = pad_rows([part], ROWS)
-    placed = jnp.concatenate([jnp.where(high == g, part, 0.0) for g in range(groups)], axis=0)
-    placed = jnp.concatenate(split(placed, 3), axis=1)
-    total_ref[...] += dot(placed, jnp.concatenate([low, low, low], axis=1), NT)
+    return scatter(part, low, one_hot(row >> 7, groups))
 
 
 def splatting(
@@ -270,19 +313,37 @@
 
     lax.fori_loop(1, cells, greet, 0)
     plan_slots(order_ref, owner_ref, row_ref, own_ref, pos_ref, ask_ref, parts_ref)
+    lookup_ref[...] = splat_table(splats_ref, sums_ref)
     pl.semaphore_wait(barrier, cells - 1)
     over_others(lambda to, source: copy(0, ask_ref, asked_ref, to, me).start())
 
-    lookup_ref[...] = splat_table(splats_ref)
-    asked_ref[me] = ask_ref[me]
-    values_ref[me] = answer(lookup_ref, asked_ref[me])
-
-    def serve(to, source):
-        copy(0, ask_ref, asked_ref, source, source).wait_recv()
-        reply_ref[source] = answer(lookup_ref, asked_ref[source])
-        copy(1, reply_ref, values_ref, source, me).start()
-
-    over_others(serve)
+    def in_groups(body):
+        size = group_of(cells)
+        body([0] + list(range(1, size)), True)
+
+        def one(i, carry):
+            body([i * size + j for j in range(size)], False)
+            return carry
+
+        lax.fori_loop(1, cells // size, one, 0)
+
+    def source_at(step):
+        return lax.rem(me + cells - step, cells)
+
+    def serve(steps, first):
+        sources = [source_at(step) for step in steps]
+        if first:
+            asked_ref[me] = ask_ref[me]
+        for source in sources[1 if first else 0 :]:
+            copy(0, ask_ref, asked_ref, source, source).wait_recv()
+        replies = [answer(lookup_ref, asked_ref[source]) for source in sources]
+        if first:
+            values_ref[me] = replies[0]
+        for source, reply in list(zip(sources, replies))[1 if first else 0 :]:
+            reply_ref[source] = reply
+            copy(1, reply_ref, values_ref, source, me).start()
+
+    in_groups(serve)
     over_others(lambda to, source: copy(1, reply_ref, values_ref, to, to).wait_recv())
     shade(
         values_ref, own_ref, pos_ref, order_ref, count_ref, target_ref, rendered_ref, out_ref,
@@ -290,15 +351,20 @@
     )
     over_others(lambda to, source: copy(2, out_ref, incoming_ref, to, me).start())
     sums_ref[...] = jnp.zeros_like(sums_ref)
-    collect(out_ref[me], asked_ref[me], sums_ref)
-
-    def receive(to, source):
-        copy(2, out_ref, incoming_ref, source, source).wait_recv()
-        collect(incoming_ref[source], asked_ref[source], sums_ref)
-
-    over_others(receive)
-    for g in range(grad_ref.shape[1] // LANES):
-        grad_ref[:, g * LANES : (g + 1) * LANES] = sums_ref[g * ROWS : g * ROWS + PARAMS, :]
+    groups = sums_ref.shape[0] // PARAMS
+
+    def receive(steps, first):
+        sources = [source_at(step) for step in steps]
+        for source in sources[1 if first else 0 :]:
+            copy(2, out_ref, incoming_ref, source, source).wait_recv()
+        parts = [incoming_ref[source] for source in sources[1 if first else 0 :]]
+        if first:
+            parts = [out_ref[me]] + parts
+        added = [collect(part, asked_ref[source], groups) for part, source in zip(parts, sources)]
+        sums_ref[...] += sum(added[1:], added[0])
+
+    in_groups(receive)
+    grad_ref[...] = sums_ref[...]
 
     def finish(to, source):
         copy(0, ask_ref, asked_ref, to, me).wait_send()
@@ -315,13 +381,14 @@
     cap = max(2, 2 * tiles * block // cells)
     order = depth_order.reshape(tiles, 8, block // 8).transpose(0, 2, 1).reshape(tiles, block)
     owner = slot_owner.reshape(tiles, block)
-    grouped = owned // LANES * ROWS
+    grouped = PARAMS * (owned // LANES)
+    pair = 2 if tiles % 2 == 0 else 1
     vmem = pltpu.VMEM
-    return pl.pallas_call(
+    rendered, grad = pl.pallas_call(
         splatting,
         out_shape=(
             jax.ShapeDtypeStruct(target.shape, F32),
-            jax.ShapeDtypeStruct((PARAMS, owned), F32),
+            jax.ShapeDtypeStruct((grouped, LANES), F32),
         ),
         in_specs=[pl.BlockSpec(memory_space=pltpu.VMEM)] * 6,
         out_specs=[pl.BlockSpec(memory_space=pltpu.VMEM)] * 2,
@@ -337,8 +404,11 @@
             vmem((2 * cells, cap), F32),
             vmem((grouped, 3 * LANES), BF16),
             vmem((grouped, LANES), F32),
-            [vmem((cells * ROWS, cap), F32), vmem((cells * ROWS, 3 * cap), BF16)]
-            + [vmem((block, PIX), F32)] * 5,
+            [
+                vmem((PARAMS * cells, cap), F32),
+                vmem((PARAMS * cells, 3 * cap), BF16),
+                [[vmem((block, PIX), F32)] * 5] * pair,
+            ],
             pltpu.SemaphoreType.DMA((3, cells)),
             pltpu.SemaphoreType.DMA((3, cells)),
         ],
@@ -346,6 +416,7 @@
             vmem_limit_bytes=48 * 1024 * 1024, collective_id=0, has_side_effects=True
         ),
     )(splats, order, owner, slot_row, tile_count.reshape(tiles, 1), target)
+    return (rendered, grad.reshape(PARAMS, owned))
 
 
 def solution(mesh):

time: 86 us -> 61.7 us (0.72)
  the two profiles are of different devices: /device:TPU:25 before, /device:TPU:13 now
where the time goes in v3:
time: 61.7 us; the launch traced here: 61.3 us
  Pallas kernels  56.9 us (92%)
  local copies, waits for them, and re-layouts  3.81 us (6%)
  between operations  0.68 us (1%)
    pallas_call x1, Pallas kernels, per_device(): pl.pallas_call(splatting, out_shape=(jax.ShapeDtypeStruct(target.shape, F...  56.9 us
    unnamed x12, local copies, waits for them, and re-layouts  2.8 us

profile of v3, /device:TPU:13, one launch (start us, length us, event | category | flops | bytes accessed | tf_op | source)
XLA Modules:
  0.0 61.3 jit_solution(1175530499471364427)
XLA Ops:
  0.6 0.0 copy-start.4
  0.6 0.6 %copy-done.4 = s32[16]{0:T(128)S(1)} copy-done((s32[16]{0:T(128)S(1)}, s32[16]{0:T(128)}, u32[]{:S(2)}) %copy-start.4) | copy-done | bytes 88
  1.3 0.1 copy.12.count_ref
  1.4 0.0 copy-start.3
  1.4 0.7 %copy.15 = s32[16,256,1]{1,0,2:T(8,128)S(1)} copy(s32[16,256,1]{1,2,0:T(1,128)} %param.8) | data formatting | bytes 32768
  2.1 0.0 copy-done.3
  2.1 0.1 reshape.19
  2.2 0.0 copy-start
  2.2 0.1 copy.10
  2.3 0.0 copy-start.1
  2.3 0.0 copy-start.2
  2.3 0.1 copy.11.order_ref
  2.4 0.7 %copy-done = f32[9,2048]{1,0:T(8,128)S(1)} copy-done((f32[9,2048]{1,0:T(8,128)S(1)}, f32[9,2048]{1,0:T(8,128)}, u32[]{:S(2)}) %copy-start) | copy-done | bytes 73752
  3.1 0.1 copy-done.1
  3.2 0.0 copy-done.2
  3.2 56.9 %shard_map.77 = (f32[3,4096]{1,0:T(4,128)S(1)}, f32[144,128]{1,0:T(8,128)S(1)}) custom-call(f32[9,2048]{1,0:T(8,128)S(1)} %copy-done, s32[16,256]{1,0:T(8,128)S(1)} %copy.11.order_ref, s32[16,256]{1,0:T(8,128)S(1)} %bitcast.7, s32[16,256]{1,0:T(8,128)S(1)} %copy-done.2, s32[16,1]{1,0:T(8,128)S(1)} %copy.12.count_ref, f32[3,4096]{1,0:T(4,128)S(1)} %copy-done.1), custom_call_target="tpu_custom_call" | custom-call | tf_op jit(solution)/shard_map/pallas_call | solution.py:387
  60.0 0.7 %reshape.23 = f32[9,2048]{1,0:T(8,128)} reshape(f32[144,128]{1,0:T(8,128)S(1)} %get-tuple-element.5) | data formatting | bytes 147456 | tf_op jit(solution)/shard_map/reshape | solution.py:419
  60.7 0.6 %copy.17 = f32[3,4096]{1,0:T(4,128)} copy(f32[3,4096]{1,0:T(4,128)S(1)} %get-tuple-element.8) | data formatting | bytes 98304
Async XLA Ops:
  0.6 0.7 %copy-start.4 = (s32[16]{0:T(128)S(1)}, s32[16]{0:T(128)}, u32[]{:S(2)}) copy-start(s32[16]{0:T(128)} %param.11) | copy-start | bytes 196
  1.4 0.7 %copy-start.3 = (s32[16,256]{1,0:T(8,128)S(1)}, s32[16,256]{1,0:T(8,128)}, u32[]{:S(2)}) copy-start(s32[16,256]{1,0:T(8,128)} %param.10) | copy-start | bytes 49156
  2.2 0.9 %copy-start = (f32[9,2048]{1,0:T(8,128)S(1)}, f32[9,2048]{1,0:T(8,128)}, u32[]{:S(2)}) copy-start(f32[9,2048]{1,0:T(8,128)} %splats_ref.1) | copy-start | bytes 221188
  2.3 0.9 %copy-start.1 = (f32[3,4096]{1,0:T(4,128)S(1)}, f32[3,4096]{1,0:T(4,128)}, u32[]{:S(2)}) copy-start(f32[3,4096]{1,0:T(4,128)} %target_ref.1) | copy-start | bytes 147460
  2.3 0.8 %copy-start.2 = (s32[16,256]{1,0:T(8,128)S(1)}, s32[16,256]{1,0:T(8,128)}, u32[]{:S(2)}) copy-start(s32[16,256]{1,0:T(8,128)} %row_ref.1) | copy-start | bytes 49156

commit v4 on v3

--- a/solution.py
+++ b/solution.py
@@ -73,9 +73,12 @@
     return dot(spread, jnp.concatenate([place, place], axis=1), NT)
 
 
-def plan_slots(order_ref, owner_ref, row_ref, own_ref, pos_ref, ask_ref, parts_ref):
+def plan_slots(depth_ref, order_ref, owner_ref, row_ref, own_ref, pos_ref, ask_ref, parts_ref):
     tiles, block = order_ref.shape
     cells, _, cap = ask_ref.shape
+    slot, place = iota((block, block), 0), iota((block, block), 1)
+    strided = jnp.where(slot == (place & 7) * (block // 8) + (place >> 3), 1.0, 0.0).astype(BF16)
+    order_ref[...] = dot(depth_ref[...].astype(F32).astype(BF16), strided).astype(I32)
     before = jnp.where(iota((block, block), 0) < iota((block, block), 1), 1.0, 0.0).astype(BF16)
     parts_ref[...] = jnp.zeros_like(parts_ref)
     group = group_of(tiles)
@@ -280,8 +283,8 @@
 
 
 def splatting(
-    splats_ref, order_ref, owner_ref, row_ref, count_ref, target_ref, rendered_ref, grad_ref,
-    own_ref, pos_ref, ask_ref, asked_ref, reply_ref, values_ref, out_ref, incoming_ref,
+    splats_ref, depth_ref, owner_ref, row_ref, count_ref, target_ref, rendered_ref, grad_ref,
+    order_ref, own_ref, pos_ref, ask_ref, asked_ref, reply_ref, values_ref, out_ref, incoming_ref,
     parts_ref, lookup_ref, sums_ref, shade_refs, send_sem, recv_sem,
 ):
     cells = ask_ref.shape[0]
@@ -312,7 +315,7 @@
         )
 
     lax.fori_loop(1, cells, greet, 0)
-    plan_slots(order_ref, owner_ref, row_ref, own_ref, pos_ref, ask_ref, parts_ref)
+    plan_slots(depth_ref, order_ref, owner_ref, row_ref, own_ref, pos_ref, ask_ref, parts_ref)
     lookup_ref[...] = splat_table(splats_ref, sums_ref)
     pl.semaphore_wait(barrier, cells - 1)
     over_others(lambda to, source: copy(0, ask_ref, asked_ref, to, me).start())
@@ -344,13 +347,15 @@
             copy(1, reply_ref, values_ref, source, me).start()
 
     in_groups(serve)
-    over_others(lambda to, source: copy(1, reply_ref, values_ref, to, to).wait_recv())
+    over_others(lambda to, source: copy(0, ask_ref, asked_ref, to, me).wait_send())
+    over_others(lambda to, source: copy(1, reply_ref, values_ref, source, source).wait_recv())
     shade(
         values_ref, own_ref, pos_ref, order_ref, count_ref, target_ref, rendered_ref, out_ref,
         *shade_refs,
     )
     over_others(lambda to, source: copy(2, out_ref, incoming_ref, to, me).start())
     sums_ref[...] = jnp.zeros_like(sums_ref)
+    over_others(lambda to, source: copy(1, reply_ref, values_ref, to, me).wait_send())
     groups = sums_ref.shape[0] // PARAMS
 
     def receive(steps, first):
@@ -366,12 +371,7 @@
     in_groups(receive)
     grad_ref[...] = sums_ref[...]
 
-    def finish(to, source):
-        copy(0, ask_ref, asked_ref, to, me).wait_send()
-        copy(1, reply_ref, values_ref, to, me).wait_send()
-        copy(2, out_ref, incoming_ref, to, me).wait_send()
-
-    over_others(finish)
+    over_others(lambda to, source: copy(2, out_ref, incoming_ref, to, me).wait_send())
 
 
 def per_device(splats, target, slot_owner, slot_row, depth_order, tile_count):
@@ -379,10 +379,8 @@
     owned = splats.shape[1]
     tiles, block = slot_row.shape
     cap = max(2, 2 * tiles * block // cells)
-    order = depth_order.reshape(tiles, 8, block // 8).transpose(0, 2, 1).reshape(tiles, block)
     owner = slot_owner.reshape(tiles, block)
     grouped = PARAMS * (owned // LANES)
-    pair = 2 if tiles % 2 == 0 else 1
     vmem = pltpu.VMEM
     rendered, grad = pl.pallas_call(
         splatting,
@@ -393,6 +391,7 @@
         in_specs=[pl.BlockSpec(memory_space=pltpu.VMEM)] * 6,
         out_specs=[pl.BlockSpec(memory_space=pltpu.VMEM)] * 2,
         scratch_shapes=[
+            vmem((tiles, block), I32),
             vmem((tiles, block), I32),
             vmem((tiles, block), I32),
             vmem((cells, 1, cap), I32),
@@ -407,7 +406,7 @@
             [
                 vmem((PARAMS * cells, cap), F32),
                 vmem((PARAMS * cells, 3 * cap), BF16),
-                [[vmem((block, PIX), F32)] * 5] * pair,
+                [[vmem((block, PIX), F32)] * 5] * group_of(tiles),
             ],
             pltpu.SemaphoreType.DMA((3, cells)),
             pltpu.SemaphoreType.DMA((3, cells)),
@@ -415,7 +414,7 @@
         compiler_params=pltpu.CompilerParams(
             vmem_limit_bytes=48 * 1024 * 1024, collective_id=0, has_side_effects=True
         ),
-    )(splats, order, owner, slot_row, tile_count.reshape(tiles, 1), target)
+    )(splats, depth_order, owner, slot_row, tile_count.reshape(tiles, 1), target)
     return (rendered, grad.reshape(PARAMS, owned))
 
 

time: 61.7 us -> 58.5 us (0.948)
  Pallas kernels: 56.9 us -> 53.1 us
  local copies, waits for them, and re-layouts: 3.81 us -> 4.52 us
    pallas_call x1, Pallas kernels: 56.9 us -> 53.1 us  [per_device(): pl.pallas_call(splatting, out_shape=(jax.ShapeDtypeStruct(target.shape, F...]
    unnamed x12, local copies, waits for them, and re-layouts: 2.8 us -> 3.77 us
where the time goes in v4:
time: 58.5 us; the launch traced here: 58.2 us
  Pallas kernels  53.1 us (91%)
  local copies, waits for them, and re-layouts  4.52 us (8%)
  between operations  0.65 us (1%)
    pallas_call x1, Pallas kernels, per_device(): pl.pallas_call(splatting, out_shape=(jax.ShapeDtypeStruct(target.shape, F...  53.1 us
    unnamed x12, local copies, waits for them, and re-layouts  3.77 us

profile of v4, /device:TPU:13, one launch (start us, length us, event | category | flops | bytes accessed | tf_op | source)
XLA Modules:
  0.0 58.2 jit_solution(10161039109710473259)
XLA Ops:
  0.6 0.0 copy-start.4
  0.6 0.6 %copy-done.4 = s32[16]{0:T(128)S(1)} copy-done((s32[16]{0:T(128)S(1)}, s32[16]{0:T(128)}, u32[]{:S(2)}) %copy-start.4) | copy-done | bytes 88
  1.3 0.1 copy.8.count_ref
  1.4 0.0 copy-start.2
  1.4 0.0 copy-start.3
  1.4 0.7 %copy.11 = s32[16,256,1]{1,0,2:T(8,128)S(1)} copy(s32[16,256,1]{1,2,0:T(1,128)} %param.8) | data formatting | bytes 32768
  2.1 0.0 copy-done.2
  2.1 0.0 copy-done.3
  2.1 0.0 copy-start
  2.1 0.9 %copy-done = f32[9,2048]{1,0:T(8,128)S(1)} copy-done((f32[9,2048]{1,0:T(8,128)S(1)}, f32[9,2048]{1,0:T(8,128)}, u32[]{:S(2)}) %copy-start) | copy-done | bytes 73752
  3.0 0.0 copy-start.1
  3.0 0.8 %copy-done.1 = f32[3,4096]{1,0:T(4,128)S(1)} copy-done((f32[3,4096]{1,0:T(4,128)S(1)}, f32[3,4096]{1,0:T(4,128)}, u32[]{:S(2)}) %copy-start.1) | copy-done | bytes 49176
  3.9 53.1 %shard_map.77 = (f32[3,4096]{1,0:T(4,128)S(1)}, f32[144,128]{1,0:T(8,128)S(1)}) custom-call(f32[9,2048]{1,0:T(8,128)S(1)} %copy-done, s32[16,256]{1,0:T(8,128)S(1)} %copy-done.2, s32[16,256]{1,0:T(8,128)S(1)} %bitcast.4, s32[16,256]{1,0:T(8,128)S(1)} %copy-done.3, s32[16,1]{1,0:T(8,128)S(1)} %copy.8.count_ref, f32[3,4096]{1,0:T(4,128)S(1)} %copy-done.1), custom_call_target="tpu_custom_call" | custom-call | tf_op jit(solution)/shard_map/pallas_call | solution.py:385
  56.9 0.7 %reshape.15 = f32[9,2048]{1,0:T(8,128)} reshape(f32[144,128]{1,0:T(8,128)S(1)} %get-tuple-element.5) | data formatting | bytes 147456 | tf_op jit(solution)/shard_map/reshape | solution.py:418
  57.6 0.6 %copy.13 = f32[3,4096]{1,0:T(4,128)} copy(f32[3,4096]{1,0:T(4,128)S(1)} %get-tuple-element.8) | data formatting | bytes 98304
Async XLA Ops:
  0.6 0.7 %copy-start.4 = (s32[16]{0:T(128)S(1)}, s32[16]{0:T(128)}, u32[]{:S(2)}) copy-start(s32[16]{0:T(128)} %param.11) | copy-start | bytes 196
  1.4 0.7 %copy-start.2 = (s32[16,256]{1,0:T(8,128)S(1)}, s32[16,256]{1,0:T(8,128)}, u32[]{:S(2)}) copy-start(s32[16,256]{1,0:T(8,128)} %depth_ref.1) | copy-start | bytes 49156
  1.4 0.7 %copy-start.3 = (s32[16,256]{1,0:T(8,128)S(1)}, s32[16,256]{1,0:T(8,128)}, u32[]{:S(2)}) copy-start(s32[16,256]{1,0:T(8,128)} %row_ref.1) | copy-start | bytes 49156
  2.1 0.9 %copy-start = (f32[9,2048]{1,0:T(8,128)S(1)}, f32[9,2048]{1,0:T(8,128)}, u32[]{:S(2)}) copy-start(f32[9,2048]{1,0:T(8,128)} %splats_ref.1) | copy-start | bytes 221188
  3.0 0.8 %copy-start.1 = (f32[3,4096]{1,0:T(4,128)S(1)}, f32[3,4096]{1,0:T(4,128)}, u32[]{:S(2)}) copy-start(f32[3,4096]{1,0:T(4,128)} %target_ref.1) | copy-start | bytes 147460

commit v5 on v4

--- a/solution.py
+++ b/solution.py
@@ -35,6 +35,11 @@
     return jnp.where(iota((count, index.shape[1]), 0) == index, 1.0, 0.0)
 
 
+def inverse(x):
+    guess = pl.reciprocal(x, approx=True)
+    return guess * (2.0 - x * guess)
+
+
 def pad_rows(pieces, count):
     have = sum(piece.shape[0] for piece in pieces)
     if have < count:
@@ -48,8 +53,8 @@
         works = [work for work in works if next(work, "end") is None]
 
 
-def group_of(count):
-    return next(size for size in (4, 2, 1) if count % size == 0)
+def group_of(count, most):
+    return next(size for size in range(most, 0, -1) if count % size == 0)
 
 
 def gather(table, place, mask):
@@ -81,7 +86,7 @@
     order_ref[...] = dot(depth_ref[...].astype(F32).astype(BF16), strided).astype(I32)
     before = jnp.where(iota((block, block), 0) < iota((block, block), 1), 1.0, 0.0).astype(BF16)
     parts_ref[...] = jnp.zeros_like(parts_ref)
-    group = group_of(tiles)
+    group = group_of(tiles, 8)
 
     def tile(t, state, asks):
         at = pl.ds(t, 1)
@@ -237,7 +242,7 @@
         for v in reversed(range(steps)):
             alpha = alpha_ref[8 * v : 8 * v + 8, :]
             u = h_ref[8 * v : 8 * v + 8, :]
-            h_ref[8 * v : 8 * v + 8, :] = u - behind * (alpha / (1.0 - alpha))
+            h_ref[8 * v : 8 * v + 8, :] = u - behind * (alpha * inverse(1.0 - alpha))
             behind = behind + u
 
         yield
@@ -321,7 +326,7 @@
     over_others(lambda to, source: copy(0, ask_ref, asked_ref, to, me).start())
 
     def in_groups(body):
-        size = group_of(cells)
+        size = group_of(cells, 8)
         body([0] + list(range(1, size)), True)
 
         def one(i, carry):
@@ -406,7 +411,7 @@
             [
                 vmem((PARAMS * cells, cap), F32),
                 vmem((PARAMS * cells, 3 * cap), BF16),
-                [[vmem((block, PIX), F32)] * 5] * group_of(tiles),
+                [[vmem((block, PIX), F32)] * 5] * group_of(tiles, 4),
             ],
             pltpu.SemaphoreType.DMA((3, cells)),
             pltpu.SemaphoreType.DMA((3, cells)),

time: 58.5 us -> 58.7 us (level); the launches traced: 58.2 us -> 57.8 us
  no operation moved by 1% of the time
where the time goes in v5:
time: 58.7 us; the launch traced here: 57.8 us
  Pallas kernels  52.6 us (90%)
  local copies, waits for them, and re-layouts  4.52 us (8%)
  between operations  0.65 us (1%)
    pallas_call x1, Pallas kernels, per_device(): pl.pallas_call(splatting, out_shape=(jax.ShapeDtypeStruct(target.shape, F...  52.6 us
    unnamed x12, local copies, waits for them, and re-layouts  3.77 us

profile of v5, /device:TPU:13, one launch (start us, length us, event | category | flops | bytes accessed | tf_op | source)
XLA Modules:
  0.0 57.8 jit_solution(16828936480144736349)
XLA Ops:
  0.6 0.0 copy-start.4
  0.6 0.6 %copy-done.4 = s32[16]{0:T(128)S(1)} copy-done((s32[16]{0:T(128)S(1)}, s32[16]{0:T(128)}, u32[]{:S(2)}) %copy-start.4) | copy-done | bytes 88
  1.3 0.1 copy.8.count_ref
  1.4 0.0 copy-start.2
  1.4 0.0 copy-start.3
  1.4 0.7 %copy.11 = s32[16,256,1]{1,0,2:T(8,128)S(1)} copy(s32[16,256,1]{1,2,0:T(1,128)} %param.8) | data formatting | bytes 32768
  2.1 0.0 copy-done.2
  2.1 0.0 copy-done.3
  2.1 0.0 copy-start
  2.1 0.9 %copy-done = f32[9,2048]{1,0:T(8,128)S(1)} copy-done((f32[9,2048]{1,0:T(8,128)S(1)}, f32[9,2048]{1,0:T(8,128)}, u32[]{:S(2)}) %copy-start) | copy-done | bytes 73752
  3.0 0.0 copy-start.1
  3.0 0.8 %copy-done.1 = f32[3,4096]{1,0:T(4,128)S(1)} copy-done((f32[3,4096]{1,0:T(4,128)S(1)}, f32[3,4096]{1,0:T(4,128)}, u32[]{:S(2)}) %copy-start.1) | copy-done | bytes 49176
  3.9 52.6 %shard_map.77 = (f32[3,4096]{1,0:T(4,128)S(1)}, f32[144,128]{1,0:T(8,128)S(1)}) custom-call(f32[9,2048]{1,0:T(8,128)S(1)} %copy-done, s32[16,256]{1,0:T(8,128)S(1)} %copy-done.2, s32[16,256]{1,0:T(8,128)S(1)} %bitcast.4, s32[16,256]{1,0:T(8,128)S(1)} %copy-done.3, s32[16,1]{1,0:T(8,128)S(1)} %copy.8.count_ref, f32[3,4096]{1,0:T(4,128)S(1)} %copy-done.1), custom_call_target="tpu_custom_call" | custom-call | tf_op jit(solution)/shard_map/pallas_call | solution.py:390
  56.5 0.7 %reshape.15 = f32[9,2048]{1,0:T(8,128)} reshape(f32[144,128]{1,0:T(8,128)S(1)} %get-tuple-element.5) | data formatting | bytes 147456 | tf_op jit(solution)/shard_map/reshape | solution.py:423
  57.1 0.6 %copy.13 = f32[3,4096]{1,0:T(4,128)} copy(f32[3,4096]{1,0:T(4,128)S(1)} %get-tuple-element.8) | data formatting | bytes 98304
Async XLA Ops:
  0.6 0.7 %copy-start.4 = (s32[16]{0:T(128)S(1)}, s32[16]{0:T(128)}, u32[]{:S(2)}) copy-start(s32[16]{0:T(128)} %param.11) | copy-start | bytes 196
  1.4 0.7 %copy-start.2 = (s32[16,256]{1,0:T(8,128)S(1)}, s32[16,256]{1,0:T(8,128)}, u32[]{:S(2)}) copy-start(s32[16,256]{1,0:T(8,128)} %depth_ref.1) | copy-start | bytes 49156
  1.4 0.7 %copy-start.3 = (s32[16,256]{1,0:T(8,128)S(1)}, s32[16,256]{1,0:T(8,128)}, u32[]{:S(2)}) copy-start(s32[16,256]{1,0:T(8,128)} %row_ref.1) | copy-start | bytes 49156
  2.1 0.9 %copy-start = (f32[9,2048]{1,0:T(8,128)S(1)}, f32[9,2048]{1,0:T(8,128)}, u32[]{:S(2)}) copy-start(f32[9,2048]{1,0:T(8,128)} %splats_ref.1) | copy-start | bytes 221188
  3.0 0.8 %copy-start.1 = (f32[3,4096]{1,0:T(4,128)S(1)}, f32[3,4096]{1,0:T(4,128)}, u32[]{:S(2)}) copy-start(f32[3,4096]{1,0:T(4,128)} %target_ref.1) | copy-start | bytes 147460

commit v6 on v5

--- a/solution.py
+++ b/solution.py
@@ -411,7 +411,7 @@
             [
                 vmem((PARAMS * cells, cap), F32),
                 vmem((PARAMS * cells, 3 * cap), BF16),
-                [[vmem((block, PIX), F32)] * 5] * group_of(tiles, 4),
+                [[vmem((block, PIX), F32)] * 5] * group_of(tiles, 8),
             ],
             pltpu.SemaphoreType.DMA((3, cells)),
             pltpu.SemaphoreType.DMA((3, cells)),

time: 58.7 us -> 58 us (0.988)
  Pallas kernels: 52.6 us -> 51.9 us
    pallas_call x1, Pallas kernels: 52.6 us -> 51.9 us  [per_device(): pl.pallas_call(splatting, out_shape=(jax.ShapeDtypeStruct(target.shape, F...]
where the time goes in v6:
time: 58 us; the launch traced here: 57 us
  Pallas kernels  51.9 us (89%)
  local copies, waits for them, and re-layouts  4.52 us (8%)
  between operations  0.65 us (1%)
    pallas_call x1, Pallas kernels, per_device(): pl.pallas_call(splatting, out_shape=(jax.ShapeDtypeStruct(target.shape, F...  51.9 us
    unnamed x12, local copies, waits for them, and re-layouts  3.77 us

profile of v6, /device:TPU:13, one launch (start us, length us, event | category | flops | bytes accessed | tf_op | source)
XLA Modules:
  0.0 57.0 jit_solution(10557415392319091003)
XLA Ops:
  0.6 0.0 copy-start.4
  0.6 0.6 %copy-done.4 = s32[16]{0:T(128)S(1)} copy-done((s32[16]{0:T(128)S(1)}, s32[16]{0:T(128)}, u32[]{:S(2)}) %copy-start.4) | copy-done | bytes 88
  1.3 0.1 copy.8.count_ref
  1.4 0.0 copy-start.2
  1.4 0.0 copy-start.3
  1.4 0.7 %copy.11 = s32[16,256,1]{1,0,2:T(8,128)S(1)} copy(s32[16,256,1]{1,2,0:T(1,128)} %param.8) | data formatting | bytes 32768
  2.1 0.0 copy-done.2
  2.1 0.0 copy-done.3
  2.1 0.0 copy-start
  2.1 0.9 %copy-done = f32[9,2048]{1,0:T(8,128)S(1)} copy-done((f32[9,2048]{1,0:T(8,128)S(1)}, f32[9,2048]{1,0:T(8,128)}, u32[]{:S(2)}) %copy-start) | copy-done | bytes 73752
  3.0 0.0 copy-start.1
  3.0 0.8 %copy-done.1 = f32[3,4096]{1,0:T(4,128)S(1)} copy-done((f32[3,4096]{1,0:T(4,128)S(1)}, f32[3,4096]{1,0:T(4,128)}, u32[]{:S(2)}) %copy-start.1) | copy-done | bytes 49176
  3.9 51.9 %shard_map.77 = (f32[3,4096]{1,0:T(4,128)S(1)}, f32[144,128]{1,0:T(8,128)S(1)}) custom-call(f32[9,2048]{1,0:T(8,128)S(1)} %copy-done, s32[16,256]{1,0:T(8,128)S(1)} %copy-done.2, s32[16,256]{1,0:T(8,128)S(1)} %bitcast.4, s32[16,256]{1,0:T(8,128)S(1)} %copy-done.3, s32[16,1]{1,0:T(8,128)S(1)} %copy.8.count_ref, f32[3,4096]{1,0:T(4,128)S(1)} %copy-done.1), custom_call_target="tpu_custom_call" | custom-call | tf_op jit(solution)/shard_map/pallas_call | solution.py:390
  55.7 0.7 %reshape.15 = f32[9,2048]{1,0:T(8,128)} reshape(f32[144,128]{1,0:T(8,128)S(1)} %get-tuple-element.5) | data formatting | bytes 147456 | tf_op jit(solution)/shard_map/reshape | solution.py:423
  56.4 0.6 %copy.13 = f32[3,4096]{1,0:T(4,128)} copy(f32[3,4096]{1,0:T(4,128)S(1)} %get-tuple-element.8) | data formatting | bytes 98304
Async XLA Ops:
  0.6 0.7 %copy-start.4 = (s32[16]{0:T(128)S(1)}, s32[16]{0:T(128)}, u32[]{:S(2)}) copy-start(s32[16]{0:T(128)} %param.11) | copy-start | bytes 196
  1.4 0.7 %copy-start.2 = (s32[16,256]{1,0:T(8,128)S(1)}, s32[16,256]{1,0:T(8,128)}, u32[]{:S(2)}) copy-start(s32[16,256]{1,0:T(8,128)} %depth_ref.1) | copy-start | bytes 49156
  1.4 0.7 %copy-start.3 = (s32[16,256]{1,0:T(8,128)S(1)}, s32[16,256]{1,0:T(8,128)}, u32[]{:S(2)}) copy-start(s32[16,256]{1,0:T(8,128)} %row_ref.1) | copy-start | bytes 49156
  2.1 0.9 %copy-start = (f32[9,2048]{1,0:T(8,128)S(1)}, f32[9,2048]{1,0:T(8,128)}, u32[]{:S(2)}) copy-start(f32[9,2048]{1,0:T(8,128)} %splats_ref.1) | copy-start | bytes 221188
  3.0 0.8 %copy-start.1 = (f32[3,4096]{1,0:T(4,128)S(1)}, f32[3,4096]{1,0:T(4,128)}, u32[]{:S(2)}) copy-start(f32[3,4096]{1,0:T(4,128)} %target_ref.1) | copy-start | bytes 147460
